TPU v7x, 32 devices: a whole 2x2x4 slice. The times are simulated.
32 devices in a mesh: src: 2 (over core), gx: 4 (over z), gy: 4 (over y, x).
Axes of the slice: x: 2, y: 2, z: 4, core: 2. Of those that a mesh axis runs over, the one named last changes fastest.
Arguments:
- forward_state: float32 [4, 6, 64, 16384], P('src', None, 'gx', 'gy'), may hold values from -6 to 6
- adjoint_state: float32 [4, 6, 64, 16384], P('src', None, 'gx', 'gy'), may hold values from -6 to 6
- permittivity: float32 [64, 16384], P('gx', 'gy'), may hold values from 1 to 3
- waveform: float32 [4, 4], P('src'), may hold values from -8 to 8
- source_cell: int32 [4, 3], P('src'), may hold values from 0 to 255, as said below
- block_owner: int32 [16, 64], P('gx', 'gy'), may hold values from -1 to 3, as said below
- block_slot: int32 [16, 64], P('gx', 'gy'), may hold values from -1 to 15, as said below
- owner_rows: int32 [16, 64], P(('gx', 'gy')), may hold values from 0 to 63, as said below
Outputs:
- design_gradient: float32 [1024, 1024], P(('gx', 'gy'), 'src')
Inputs may be any that keep to these rules, and one draw needn't show every extreme that they name: `block_owner`: -1 marks a block outside the design region; otherwise the owner lies in the block's own gx row. The design blocks of one device that go to one owner number at most 16, and some device sends exactly 16 to some owner. `block_slot`: -1 exactly where block_owner is -1; the blocks that one device sends to one owner have distinct slots. `owner_rows`: each row is a permutation of 0 to 63. `source_cell`: each row is a cell (x, y, z) of the grid.
All inputs are finite; a program needn't handle non-finite values.
Results may differ from a plain program's by a relative error of at most 0.0003.
Values sent between devices are 32-bit elements; how exact they have to be, the bound alone decides.
A program may use at most 128 MiB of HBM per device.

v0:
```python
import jax
import jax.numpy as jnp
from jax import lax
from jax.sharding import PartitionSpec as P

NZ = 64
STEPS = 4
BX = 4
BY = 4


courant = 0.55


def passed_along(shard, axis, by):
    count = lax.axis_size(axis)
    pairs = [(i, i + by) for i in range(count) if 0 <= i + by < count]
    return lax.ppermute(shard, axis, pairs)


def upper_z(values, z_cells):
    zindex = lax.broadcasted_iota(jnp.int32, values.shape, values.ndim - 1) % z_cells
    shifted = jnp.concatenate([values[..., 1:], jnp.zeros_like(values[..., :1])], axis=-1)
    return jnp.where(zindex == z_cells - 1, jnp.zeros_like(shifted), shifted)


def lower_z(values, z_cells):
    zindex = lax.broadcasted_iota(jnp.int32, values.shape, values.ndim - 1) % z_cells
    shifted = jnp.concatenate([jnp.zeros_like(values[..., :1]), values[..., :-1]], axis=-1)
    return jnp.where(zindex == 0, jnp.zeros_like(shifted), shifted)


def upper_x(values, ghosts):
    return jnp.concatenate([values[..., 1:, :], ghosts], axis=-2)


def lower_x(values, ghosts):
    return jnp.concatenate([ghosts, values[..., :-1, :]], axis=-2)


def upper_y(values, ghosts, z_cells):
    return jnp.concatenate([values[..., z_cells:], ghosts], axis=-1)


def lower_y(values, ghosts, z_cells):
    return jnp.concatenate([ghosts, values[..., :-z_cells]], axis=-1)


def magnetic_update(electric, magnetic, ghost_x, ghost_y, z_cells):
    new_hx = magnetic[0] - courant * (
        upper_y(electric[2], ghost_y[1], z_cells)
        - electric[2]
        - (upper_z(electric[1], z_cells) - electric[1])
    )
    new_hy = magnetic[1] - courant * (
        upper_z(electric[0], z_cells)
        - electric[0]
        - (upper_x(electric[2], ghost_x[1]) - electric[2])
    )
    new_hz = magnetic[2] - courant * (
        upper_x(electric[1], ghost_x[0])
        - electric[1]
        - (upper_y(electric[0], ghost_y[0], z_cells) - electric[0])
    )
    return (new_hx, new_hy, new_hz)


def electric_update(electric, magnetic, ghost_x, ghost_y, factor, z_cells):
    new_ex = electric[0] + factor * (
        magnetic[2]
        - lower_y(magnetic[2], ghost_y[1], z_cells)
        - (magnetic[1] - lower_z(magnetic[1], z_cells))
    )
    new_ey = electric[1] + factor * (
        magnetic[0]
        - lower_z(magnetic[0], z_cells)
        - (magnetic[2] - lower_x(magnetic[2], ghost_x[1]))
    )
    new_ez = electric[2] + factor * (
        magnetic[1]
        - lower_x(magnetic[1], ghost_x[0])
        - (magnetic[0] - lower_y(magnetic[0], ghost_y[0], z_cells))
    )
    return (new_ex, new_ey, new_ez)


def upper_ghosts(electric, z_cells):
    planes = jnp.stack([electric[1][:, :1, :], electric[2][:, :1, :]], axis=1)
    planes = passed_along(planes, "gx", -1)
    strips = jnp.stack([electric[0][..., :z_cells], electric[2][..., :z_cells]], axis=1)
    flat_strips = passed_along(strips.reshape(strips.shape[0], 2, -1), "gy", -1)
    strips = flat_strips.reshape(strips.shape)
    return ((planes[:, 0], planes[:, 1]), (strips[:, 0], strips[:, 1]))


def lower_ghosts(magnetic, z_cells):
    planes = jnp.stack([magnetic[1][:, -1:, :], magnetic[2][:, -1:, :]], axis=1)
    planes = passed_along(planes, "gx", 1)
    strips = jnp.stack([magnetic[0][..., -z_cells:], magnetic[2][..., -z_cells:]], axis=1)
    flat_strips = passed_along(strips.reshape(strips.shape[0], 2, -1), "gy", 1)
    strips = flat_strips.reshape(strips.shape)
    return ((planes[:, 0], planes[:, 1]), (strips[:, 0], strips[:, 1]))


def advance(electric, magnetic, factor, z_cells):
    ghost_x, ghost_y = upper_ghosts(electric, z_cells)
    magnetic = magnetic_update(electric, magnetic, ghost_x, ghost_y, z_cells)
    ghost_x, ghost_y = lower_ghosts(magnetic, z_cells)
    electric = electric_update(electric, magnetic, ghost_x, ghost_y, factor, z_cells)
    return (electric, magnetic)


def per_device(
    forward_state,
    adjoint_state,
    permittivity,
    waveform,
    source_cell,
    block_owner,
    block_slot,
    owner_rows,
):
    cells_x = permittivity.shape[0]
    cells_yz = permittivity.shape[1]
    cells_y = cells_yz // NZ
    factor = courant / permittivity
    x_index = lax.broadcasted_iota(jnp.int32, (cells_x, cells_yz), 0)
    yz_index = lax.broadcasted_iota(jnp.int32, (cells_x, cells_yz), 1)
    local_x = source_cell[:, 0] - lax.axis_index("gx") * cells_x
    local_yz = (source_cell[:, 1] - lax.axis_index("gy") * cells_y) * NZ + source_cell[:, 2]
    beacon = (
        (x_index[None] == local_x[:, None, None]) & (yz_index[None] == local_yz[:, None, None])
    ).astype(jnp.float32)
    density = jnp.zeros((cells_x, cells_yz), jnp.float32)
    electric = (forward_state[:, 0], forward_state[:, 1], forward_state[:, 2])
    magnetic = (forward_state[:, 3], forward_state[:, 4], forward_state[:, 5])
    increments = []
    for step_index in range(STEPS):
        updated, magnetic = advance(electric, magnetic, factor, NZ)
        updated = (
            updated[0],
            updated[1],
            updated[2] + waveform[:, step_index][:, None, None] * beacon,
        )
        increments.append(
            (updated[0] - electric[0], updated[1] - electric[1], updated[2] - electric[2])
        )
        electric = updated
    electric = (adjoint_state[:, 0], adjoint_state[:, 1], adjoint_state[:, 2])
    magnetic = (adjoint_state[:, 3], adjoint_state[:, 4], adjoint_state[:, 5])
    for step_index in range(STEPS):
        electric, magnetic = advance(electric, magnetic, factor, NZ)
        paired = increments[STEPS - 1 - step_index]
        intersection = electric[0] * paired[0] + electric[1] * paired[1] + electric[2] * paired[2]
        density = density + jnp.sum(intersection, axis=0)
    gradient = -density / permittivity
    blocks = (
        gradient.reshape(cells_x // BX, BX, cells_y // BY, BY, NZ)
        .transpose(0, 2, 1, 3, 4)
        .reshape(-1, BX * BY * NZ)
    )
    owners = block_owner.reshape(-1)
    slots = block_slot.reshape(-1)
    peers = lax.axis_size("gy")
    capacity = max(2, (blocks.shape[0] + peers - 1) // peers)
    rows_owned = peers * capacity
    destination = jnp.where(owners >= 0, owners * capacity + slots, rows_owned)
    outgoing = (
        jnp.zeros((rows_owned, blocks.shape[1]), jnp.float32)
        .at[destination]
        .set(blocks, mode="drop")
    )
    sectioned = outgoing.reshape(peers, capacity, 1, -1)
    arrived = lax.all_to_all(
        lax.all_to_all(sectioned, "src", split_axis=3, concat_axis=2, tiled=True),
        "gy",
        split_axis=0,
        concat_axis=0,
        tiled=True,
    )
    arrived = jnp.sum(arrived, axis=2)
    placed = jnp.zeros((rows_owned, arrived.shape[-1]), jnp.float32)
    return placed.at[owner_rows[0]].set(arrived.reshape(rows_owned, -1))


def solution(mesh):
    in_specs = (
        P("src", None, "gx", "gy"),
        P("src", None, "gx", "gy"),
        P("gx", "gy"),
        P("src", None),
        P("src", None),
        P("gx", "gy"),
        P("gx", "gy"),
        P(("gx", "gy"), None),
    )
    out_specs = P(("gx", "gy"), "src")
    return jax.shard_map(
        per_device, mesh=mesh, in_specs=in_specs, out_specs=out_specs, check_vma=False
    )
```

profile of v0, /device:TPU:0, one launch (start us, length us, event | category | flops | bytes accessed | tf_op | source)
XLA Modules:
  0.0 344.8 jit_solution(6446340232249380745)
XLA Ops:
  0.0 1.5 slice_bitcast_fusion.2
  5.0 1.5 slice_bitcast_fusion.5
  25.7 1.8 fusion.173
  29.3 1.5 fusion.170
  33.6 6.7 %collective-permute-start.5 = (f32[2,2,1024]{2,0,1:T(2,128)}, f32[2,2,1024]{2,0,1:T(2,128)}, u32[]{:S(2)}, u32[]{:S(2)}) collective-permute-start(f32[2,2,1024]{2,0,1:T(2,128)} %pad_maximum_fusion.19), channel_id=1, source_target_pairs={{0,1},{1,2},{2,3},{4,5},{5,6},{6,7},{8,9},{9,10},{10,11},{12,13},{... | collective-permute-start | bytes 49160 | tf_op jit(solution)/shard_map/ppermute | solution.py:18
  41.0 5.9 %collective-permute-start.6 = (f32[2,2,1,4096]{3,1,2,0:T(2,128)}, f32[2,2,1,4096]{3,1,2,0:T(2,128)}, u32[]{:S(2)}, u32[]{:S(2)}) collective-permute-start(f32[2,2,1,4096]{3,1,2,0:T(2,128)} %pad_maximum_fusion.2), channel_id=1, source_target_pairs={{0,4},{4,8},{8,12},{1,5},{5,9},{9,13},{2,6},{6,10},{10,14},{3,7},{... | collective-permute-start | bytes 196616 | tf_op jit(solution)/shard_map/ppermute | solution.py:18
  46.9 2.7 fusion.102
  50.5 3.9 %collective-permute-start.18 = (f32[2,2,1,4096]{3,1,2,0:T(2,128)}, f32[2,2,1,4096]{3,1,2,0:T(2,128)}, u32[]{:S(2)}, u32[]{:S(2)}) collective-permute-start(f32[2,2,1,4096]{3,1,2,0:T(2,128)} %pad_maximum_fusion.8), channel_id=1, source_target_pairs={{0,4},{4,8},{8,12},{1,5},{5,9},{9,13},{2,6},{6,10},{10,14},{3,7},{... | collective-permute-start | bytes 196616 | tf_op jit(solution)/shard_map/ppermute | solution.py:18
  55.4 4.2 %collective-permute-start.2 = (f32[2,2,1024]{2,0,1:T(2,128)S(1)}, f32[2,2,1024]{2,0,1:T(2,128)S(1)}, u32[]{:S(2)}, u32[]{:S(2)}) collective-permute-start(f32[2,2,1024]{2,0,1:T(2,128)S(1)} %pad_maximum_fusion.17), channel_id=1, source_target_pairs={{0,1},{1,2},{2,3},{4,5},{5,6},{6,7},{8,9},{9,10},{10,11},{12,13},{... | collective-permute-start | bytes 49160 | tf_op jit(solution)/shard_map/ppermute | solution.py:18
  64.2 1.7 fusion.43
  75.5 4.8 %collective-permute-done.7 = f32[2,2,1,4096]{3,1,2,0:T(2,128)S(1)} collective-permute-done((f32[2,2,1,4096]{3,1,2,0:T(2,128)S(1)}, f32[2,2,1,4096]{3,1,2,0:T(2,128)S(1)}, u32[]{:S(2)}, u32[]{:S(2)}) %collective-permute-start.7) | collective-permute-done | bytes 65568 | tf_op jit(solution)/shard_map/ppermute | solution.py:18
  80.3 2.5 fusion.118
  84.1 4.8 %collective-permute-start.9 = (f32[2,2,1024]{2,0,1:T(2,128)S(1)}, f32[2,2,1024]{2,0,1:T(2,128)S(1)}, u32[]{:S(2)}, u32[]{:S(2)}) collective-permute-start(f32[2,2,1024]{2,0,1:T(2,128)S(1)} %pad_maximum_fusion.21), channel_id=1, source_target_pairs={{0,1},{1,2},{2,3},{4,5},{5,6},{6,7},{8,9},{9,10},{10,11},{12,13},{... | collective-permute-start | bytes 49160 | tf_op jit(solution)/shard_map/ppermute | solution.py:18
  89.0 3.9 %collective-permute-start.10 = (f32[2,2,1,4096]{3,1,2,0:T(2,128)S(1)}, f32[2,2,1,4096]{3,1,2,0:T(2,128)S(1)}, u32[]{:S(2)}, u32[]{:S(2)}) collective-permute-start(f32[2,2,1,4096]{3,1,2,0:T(2,128)S(1)} %pad_maximum_fusion.4), channel_id=1, source_target_pairs={{0,4},{4,8},{8,12},{1,5},{5,9},{9,13},{2,6},{6,10},{10,14},{3,7},{... | collective-permute-start | bytes 196616 | tf_op jit(solution)/shard_map/ppermute | solution.py:18
  93.1 1.8 collective-permute-done.10
  94.9 1.5 fusion.184
  104.6 1.5 pad_maximum_fusion.5
  114.0 4.7 %collective-permute-done.11 = f32[2,2,1,4096]{3,1,2,0:T(2,128)} collective-permute-done((f32[2,2,1,4096]{3,1,2,0:T(2,128)}, f32[2,2,1,4096]{3,1,2,0:T(2,128)}, u32[]{:S(2)}, u32[]{:S(2)}) %collective-permute-start.11) | collective-permute-done | bytes 65568 | tf_op jit(solution)/shard_map/ppermute | solution.py:18
  119.7 3.6 %fusion.126 = (f32[2,16,4096]{2,1,0:T(8,128)S(1)}, f32[2,16,4096]{2,1,0:T(8,128)}, f32[2,16,4096]{2,1,0:T(8,128)S(1)}) fusion(f32[2,16,4096]{2,1,0:T(8,128)} %copy-done.9, f32[2,16,4096]{2,1,0:T(8,128)S(1)} %get-tuple-element.36, f32[2,16,4096]{2,1,0:T(8,128)S(1)} %fusion.184, f32[2,16,64]{2,1,0:T(8,128)S(1)} %get-tuple-element.110, ...), kind=kLoop, calls=%fused_computation.132 | loop fusion | flops 3014656 | bytes 7900928 | tf_op jit(solution)/shard_map/sub | solution.py:50
  124.5 5.5 %collective-permute-start.13 = (f32[2,2,1024]{2,0,1:T(2,128)S(1)}, f32[2,2,1024]{2,0,1:T(2,128)S(1)}, u32[]{:S(2)}, u32[]{:S(2)}) collective-permute-start(f32[2,2,1024]{2,0,1:T(2,128)S(1)} %pad_maximum_fusion.23), channel_id=1, source_target_pairs={{0,1},{1,2},{2,3},{4,5},{5,6},{6,7},{8,9},{9,10},{10,11},{12,13},{... | collective-permute-start | bytes 49160 | tf_op jit(solution)/shard_map/ppermute | solution.py:18
  131.0 3.9 %collective-permute-start.14 = (f32[2,2,1,4096]{3,1,2,0:T(2,128)S(1)}, f32[2,2,1,4096]{3,1,2,0:T(2,128)S(1)}, u32[]{:S(2)}, u32[]{:S(2)}) collective-permute-start(f32[2,2,1,4096]{3,1,2,0:T(2,128)S(1)} %pad_maximum_fusion.6), channel_id=1, source_target_pairs={{0,4},{4,8},{8,12},{1,5},{5,9},{9,13},{2,6},{6,10},{10,14},{3,7},{... | collective-permute-start | bytes 196616 | tf_op jit(solution)/shard_map/ppermute | solution.py:18
  135.1 1.8 collective-permute-done.14
  136.9 1.8 fusion.191
  139.4 2.3 fusion.59
  146.6 1.5 collective-permute-start.16
  148.1 1.5 pad_maximum_fusion.7
  157.4 4.7 %collective-permute-done.15 = f32[2,2,1,4096]{3,1,2,0:T(2,128)} collective-permute-done((f32[2,2,1,4096]{3,1,2,0:T(2,128)}, f32[2,2,1,4096]{3,1,2,0:T(2,128)}, u32[]{:S(2)}, u32[]{:S(2)}) %collective-permute-start.15) | collective-permute-done | bytes 65568 | tf_op jit(solution)/shard_map/ppermute | solution.py:18
  163.1 3.0 fusion.134
  171.8 6.0 %collective-permute-start.17 = (f32[2,2,1024]{2,0,1:T(2,128)S(1)}, f32[2,2,1024]{2,0,1:T(2,128)}, u32[]{:S(2)}, u32[]{:S(2)}) collective-permute-start(f32[2,2,1024]{2,0,1:T(2,128)S(1)} %pad_maximum_fusion.25), channel_id=1, source_target_pairs={{0,1},{1,2},{2,3},{4,5},{5,6},{6,7},{8,9},{9,10},{10,11},{12,13},{... | collective-permute-start | bytes 49160 | tf_op jit(solution)/shard_map/ppermute | solution.py:18
  177.8 1.4 pad_maximum_fusion.9
  179.3 4.5 %collective-permute-start.19 = (f32[2,2,1,4096]{3,1,2,0:T(2,128)}, f32[2,2,1,4096]{3,1,2,0:T(2,128)}, u32[]{:S(2)}, u32[]{:S(2)}) collective-permute-start(f32[2,2,1,4096]{3,1,2,0:T(2,128)} %pad_maximum_fusion.9), channel_id=1, source_target_pairs={{0,4},{4,8},{8,12},{1,5},{5,9},{9,13},{2,6},{6,10},{10,14},{3,7},{... | collective-permute-start | bytes 196616 | tf_op jit(solution)/shard_map/ppermute | solution.py:18
  186.4 6.4 %fusion.166 = (f32[16,4096]{1,0:T(8,128)}, f32[2,16,4096]{2,1,0:T(8,128)S(1)}, f32[2,16,4096]{2,1,0:T(8,128)S(1)}, f32[2,16,4096]{2,1,0:T(8,128)S(1)}) fusion(f32[2,16,4096]{2,1,0:T(8,128)} %get-tuple-element.35, f32[2,16,4096]{2,1,0:T(8,128)} %copy-done.48, f32[2,16,4096]{2,1,0:T(8,128)S(1)} %get-tuple-element.34, f32[2,16,4096]{2,1,0:T(8,128)} %copy-done.50, ...), kind=kLoop, calls=%fused_computation.172 | loop fusion | flops 7536640 | bytes 14716440 | tf_op jit(solution)/shard_map/reduce_sum | solution.py:155
  196.2 1.9 slice.1112
  198.1 2.0 slice.1116
  200.1 2.0 slice.1120
  207.2 4.6 %collective-permute-done.20 = f32[2,2,1,4096]{3,1,2,0:T(2,128)S(1)} collective-permute-done((f32[2,2,1,4096]{3,1,2,0:T(2,128)}, f32[2,2,1,4096]{3,1,2,0:T(2,128)S(1)}, u32[]{:S(2)}, u32[]{:S(2)}) %collective-permute-start.20) | collective-permute-done | bytes 65568 | tf_op jit(solution)/shard_map/ppermute | solution.py:18
  211.9 4.1 %fusion.142 = (f32[2,16,4096]{2,1,0:T(8,128)S(1)}, f32[2,16,4096]{2,1,0:T(8,128)}, f32[2,16,4096]{2,1,0:T(8,128)S(1)}) fusion(f32[2,16,4096]{2,1,0:T(8,128)} %copy-done.37, f32[2,16,4096]{2,1,0:T(8,128)} %copy-done.33, f32[2,16,4096]{2,1,0:T(8,128)} %copy-done.20, f32[2,16,64]{2,1,0:T(8,128)S(1)} %get-tuple-element.98, f32[2,16,4032]{2,1,0:T(8,128)} %slice.1120, ...), kind=kLoop, calls=%fused_computation.148 | loop fusion | flops 3014656 | bytes 7900928 | tf_op jit(solution)/shard_map/sub | solution.py:50
  217.2 5.5 %collective-permute-start.22 = (f32[2,2,1024]{2,0,1:T(2,128)S(1)}, f32[2,2,1024]{2,0,1:T(2,128)}, u32[]{:S(2)}, u32[]{:S(2)}) collective-permute-start(f32[2,2,1024]{2,0,1:T(2,128)S(1)} %pad_maximum_fusion.27), channel_id=1, source_target_pairs={{0,1},{1,2},{2,3},{4,5},{5,6},{6,7},{8,9},{9,10},{10,11},{12,13},{... | collective-permute-start | bytes 49160 | tf_op jit(solution)/shard_map/ppermute | solution.py:18
  224.3 3.9 %collective-permute-start.23 = (f32[2,2,1,4096]{3,1,2,0:T(2,128)}, f32[2,2,1,4096]{3,1,2,0:T(2,128)S(1)}, u32[]{:S(2)}, u32[]{:S(2)}) collective-permute-start(f32[2,2,1,4096]{3,1,2,0:T(2,128)} %pad_maximum_fusion.11), channel_id=1, source_target_pairs={{0,4},{4,8},{8,12},{1,5},{5,9},{9,13},{2,6},{6,10},{10,14},{3,7},{... | collective-permute-start | bytes 196616 | tf_op jit(solution)/shard_map/ppermute | solution.py:18
  230.5 1.9 fusion.209
  237.1 1.9 slice.1140
  238.9 2.0 slice.1144
  241.0 2.0 slice.1150
  248.1 4.5 %collective-permute-done.24 = f32[2,2,1,4096]{3,1,2,0:T(2,128)S(1)} collective-permute-done((f32[2,2,1,4096]{3,1,2,0:T(2,128)}, f32[2,2,1,4096]{3,1,2,0:T(2,128)S(1)}, u32[]{:S(2)}, u32[]{:S(2)}) %collective-permute-start.24) | collective-permute-done | bytes 65568 | tf_op jit(solution)/shard_map/ppermute | solution.py:18
  252.6 4.1 %fusion.150 = (f32[2,16,4096]{2,1,0:T(8,128)S(1)}, f32[2,16,4096]{2,1,0:T(8,128)}, f32[2,16,4096]{2,1,0:T(8,128)S(1)}) fusion(f32[2,16,4096]{2,1,0:T(8,128)} %copy-done.7, f32[2,16,4096]{2,1,0:T(8,128)} %copy-done.36, f32[2,16,4096]{2,1,0:T(8,128)} %copy-done.18, f32[2,16,64]{2,1,0:T(8,128)S(1)} %get-tuple-element.94, f32[2,16,4032]{2,1,0:T(8,128)} %slice.1148, ...), kind=kLoop, calls=%fused_computation.156 | loop fusion | flops 3014656 | bytes 7900928 | tf_op jit(solution)/shard_map/sub | solution.py:50
  258.0 5.5 %collective-permute-start.26 = (f32[2,2,1024]{2,0,1:T(2,128)S(1)}, f32[2,2,1024]{2,0,1:T(2,128)}, u32[]{:S(2)}, u32[]{:S(2)}) collective-permute-start(f32[2,2,1024]{2,0,1:T(2,128)S(1)} %pad_maximum_fusion.29), channel_id=1, source_target_pairs={{0,1},{1,2},{2,3},{4,5},{5,6},{6,7},{8,9},{9,10},{10,11},{12,13},{... | collective-permute-start | bytes 49160 | tf_op jit(solution)/shard_map/ppermute | solution.py:18
  265.1 3.9 %collective-permute-start.27 = (f32[2,2,1,4096]{3,1,2,0:T(2,128)}, f32[2,2,1,4096]{3,1,2,0:T(2,128)S(1)}, u32[]{:S(2)}, u32[]{:S(2)}) collective-permute-start(f32[2,2,1,4096]{3,1,2,0:T(2,128)} %pad_maximum_fusion.13), channel_id=1, source_target_pairs={{0,4},{4,8},{8,12},{1,5},{5,9},{9,13},{2,6},{6,10},{10,14},{3,7},{... | collective-permute-start | bytes 196616 | tf_op jit(solution)/shard_map/ppermute | solution.py:18
  271.3 5.4 %add_reduce_fusion.1 = (f32[16,4096]{1,0:T(8,128)}, f32[16,4096]{1,0:T(8,128)}, f32[2,16,4096]{2,1,0:T(8,128)S(1)}, f32[2,16,4096]{2,1,0:T(8,128)S(1)}, f32[2,16,4096]{2,1,0:T(8,128)S(1)}) fusion(f32[2,16,4096]{2,1,0:T(8,128)} %copy-done.18, f32[2,16,4096]{2,1,0:T(8,128)S(1)} %fusion.191, f32[2,16,4096]{2,1,0:T(8,128)S(1)} %fusion.184, ...), kind=kLoop, calls=%fused_computation.295 | loop fusion | flops 5242880 | bytes 13405952 | tf_op jit(solution)/shard_map/reduce_sum | solution.py:155
  279.5 2.0 slice.1168
  281.5 2.0 slice.1172
  283.5 2.0 slice.1176
  290.5 4.4 %collective-permute-done.28 = f32[2,2,1,4096]{3,1,2,0:T(2,128)} collective-permute-done((f32[2,2,1,4096]{3,1,2,0:T(2,128)S(1)}, f32[2,2,1,4096]{3,1,2,0:T(2,128)}, u32[]{:S(2)}, u32[]{:S(2)}) %collective-permute-start.28) | collective-permute-done | bytes 65568 | tf_op jit(solution)/shard_map/ppermute | solution.py:18
  295.9 2.8 fusion.158
  300.1 4.9 %collective-permute-start.30 = (f32[2,2,1024]{2,0,1:T(2,128)S(1)}, f32[2,2,1024]{2,0,1:T(2,128)S(1)}, u32[]{:S(2)}, u32[]{:S(2)}) collective-permute-start(f32[2,2,1024]{2,0,1:T(2,128)S(1)} %pad_maximum_fusion.31), channel_id=1, source_target_pairs={{0,1},{1,2},{2,3},{4,5},{5,6},{6,7},{8,9},{9,10},{10,11},{12,13},{... | collective-permute-start | bytes 49160 | tf_op jit(solution)/shard_map/ppermute | solution.py:18
  305.0 4.1 %collective-permute-start.31 = (f32[2,2,1,4096]{3,1,2,0:T(2,128)S(1)}, f32[2,2,1,4096]{3,1,2,0:T(2,128)S(1)}, u32[]{:S(2)}, u32[]{:S(2)}) collective-permute-start(f32[2,2,1,4096]{3,1,2,0:T(2,128)S(1)} %pad_maximum_fusion.15), channel_id=1, source_target_pairs={{0,4},{4,8},{8,12},{1,5},{5,9},{9,13},{2,6},{6,10},{10,14},{3,7},{... | collective-permute-start | bytes 196616 | tf_op jit(solution)/shard_map/ppermute | solution.py:18
  309.3 1.6 collective-permute-done.31
  310.9 4.2 %fusion.93 = f32[16,4096]{1,0:T(8,128)S(1)} fusion(f32[2,16,4096]{2,1,0:T(8,128)} %copy-done.39, f32[2,16,4096]{2,1,0:T(8,128)} %copy-done.49, f32[2,16,4096]{2,1,0:T(8,128)} %copy-done.31, f32[2,16,4096]{2,1,0:T(8,128)} %copy-done.51, f32[2,16,4096]{2,1,0:T(8,128)} %copy-done.47, f32[2,16,4032]{2,1,0:T(8,128)} %bitcast.415, ...), kind=kLoop, calls=%fused_computation.99 | loop fusion | flops 4128768 | bytes 9998080 | tf_op jit(solution)/shard_map/reduce_sum | solution.py:155
  317.2 1.7 copy.85
  318.9 2.9 reshape.295
  321.8 3.9 %all_to_all.17 = f32[2,1,32768]{2,1,0:T(1,128)S(1)} all-to-all(f32[2,1,32768]{2,1,0:T(1,128)S(1)} %reshape.295), channel_id=1, replica_groups=mesh['src'=2,'gx'=4,'gy'=4] {'src'}, dimensions={0} | all-to-all | bytes 524288 | tf_op jit(solution)/shard_map/all_to_all | solution.py:175
  327.7 2.8 reshape.296
  330.5 2.5 copy.86
  333.0 4.2 %all-to-all-start.1 = ((f32[4,16,2,512]{3,1,2,0:T(8,128)}), f32[4,16,2,512]{3,1,2,0:T(8,128)S(1)}, u32[]{:S(2)}, u32[]{:S(2)}) async-start(f32[4,16,2,512]{3,1,2,0:T(8,128)} %copy.86), calls=%async_computation.1 | async-start | bytes 524288 | tf_op jit(solution)/shard_map/all_to_all | solution.py:174
  337.2 6.1 %all-to-all-done.1 = f32[4,16,2,512]{3,1,2,0:T(8,128)S(1)} async-done(((f32[4,16,2,512]{3,1,2,0:T(8,128)}), f32[4,16,2,512]{3,1,2,0:T(8,128)S(1)}, u32[]{:S(2)}, u32[]{:S(2)}) %all-to-all-start.1) | async-done | bytes 262176 | tf_op jit(solution)/shard_map/all_to_all | solution.py:174
  (417 shorter events, 131.1 us)
Async XLA Ops:
  0.0 11.1 %copy-start.63 = (f32[2,4]{1,0:T(2,128)S(1)}, f32[2,4]{1,0:T(2,128)}, u32[]{:S(2)}) copy-start(f32[2,4]{1,0:T(2,128)} %param.11) | copy-start | bytes 100
  0.0 11.9 %copy-start.68 = (s32[4,16]{1,0:T(4,128)S(1)}, s32[4,16]{1,0:T(4,128)}, u32[]{:S(2)}) copy-start(s32[4,16]{1,0:T(4,128)} %param.13) | copy-start | bytes 772
  0.0 11.9 %copy-start.67 = (s32[4,16]{1,0:T(4,128)S(1)}, s32[4,16]{1,0:T(4,128)}, u32[]{:S(2)}) copy-start(s32[4,16]{1,0:T(4,128)} %param.14) | copy-start | bytes 772
  0.0 12.6 %copy-start.66 = (s32[2,3]{1,0:T(2,128)S(1)}, s32[2,3]{1,0:T(2,128)}, u32[]{:S(2)}) copy-start(s32[2,3]{1,0:T(2,128)} %param.12) | copy-start | bytes 76
  2.3 22.4 %collective-permute-start.3 = (f32[2,2,1,4096]{3,1,2,0:T(2,128)}, f32[2,2,1,4096]{3,1,2,0:T(2,128)}, u32[]{:S(2)}, u32[]{:S(2)}) collective-permute-start(f32[2,2,1,4096]{3,1,2,0:T(2,128)} %pad_maximum_fusion.1), channel_id=1, source_target_pairs={{4,0},{8,4},{12,8},{5,1},{9,5},{13,9},{6,2},{10,6},{14,10},{7,3},{... | collective-permute-start | bytes 196616 | tf_op jit(solution)/shard_map/ppermute | solution.py:18
  3.7 19.6 %collective-permute-start.4 = (f32[2,2,1024]{2,0,1:T(2,128)S(1)}, f32[2,2,1024]{2,0,1:T(2,128)S(1)}, u32[]{:S(2)}, u32[]{:S(2)}) collective-permute-start(f32[2,2,1024]{2,0,1:T(2,128)S(1)} %pad_maximum_fusion.18), channel_id=1, source_target_pairs={{1,0},{2,1},{3,2},{5,4},{6,5},{7,6},{9,8},{10,9},{11,10},{13,12},{... | collective-permute-start | bytes 49160 | tf_op jit(solution)/shard_map/ppermute | solution.py:18
  7.2 21.1 %collective-permute-start = (f32[2,2,1,4096]{3,1,2,0:T(2,128)}, f32[2,2,1,4096]{3,1,2,0:T(2,128)}, u32[]{:S(2)}, u32[]{:S(2)}) collective-permute-start(f32[2,2,1,4096]{3,1,2,0:T(2,128)} %pad_maximum_fusion), channel_id=1, source_target_pairs={{4,0},{8,4},{12,8},{5,1},{9,5},{13,9},{6,2},{10,6},{14,10},{7,3},{... | collective-permute-start | bytes 196616 | tf_op jit(solution)/shard_map/ppermute | solution.py:18
  8.7 15.3 %collective-permute-start.1 = (f32[2,2,1024]{2,0,1:T(2,128)S(1)}, f32[2,2,1024]{2,0,1:T(2,128)S(1)}, u32[]{:S(2)}, u32[]{:S(2)}) collective-permute-start(f32[2,2,1024]{2,0,1:T(2,128)S(1)} %pad_maximum_fusion.16), channel_id=1, source_target_pairs={{1,0},{2,1},{3,2},{5,4},{6,5},{7,6},{9,8},{10,9},{11,10},{13,12},{... | collective-permute-start | bytes 49160 | tf_op jit(solution)/shard_map/ppermute | solution.py:18
  12.8 82.2 %copy-start.64 = (s32[2]{0:T(128)}, s32[2]{0:T(128)S(1)}, u32[]{:S(2)}) copy-start(s32[2]{0:T(128)S(1)} %get-tuple-element.12) | copy-start | bytes 28
  22.3 7.0 %copy-start.56 = (f32[2,15,4096]{2,1,0:T(8,128)S(1)}, f32[2,15,4096]{2,1,0:T(8,128)}, u32[]{:S(2)}) copy-start(f32[2,15,4096]{2,1,0:T(8,128)} %slice.972) | copy-start | bytes 1474564
  23.3 6.0 %copy-start.57 = (f32[2,16,4032]{2,1,0:T(8,128)S(1)}, f32[2,16,4032]{2,1,0:T(8,128)}, u32[]{:S(2)}) copy-start(f32[2,16,4032]{2,1,0:T(8,128)} %slice.976) | copy-start | bytes 1548292
  25.7 6.0 %copy-start = (f32[2,6,16,4096]{3,2,1,0:T(8,128)S(1)}, f32[2,6,16,4096]{3,2,1,0:T(8,128)}, u32[]{:S(2)}) copy-start(f32[2,6,16,4096]{3,2,1,0:T(8,128)} %param.8) | copy-start | bytes 9437188
  25.7 6.0 %copy-start.52 = (f32[2,15,4096]{2,1,0:T(8,128)S(1)}, f32[2,15,4096]{2,1,0:T(8,128)}, u32[]{:S(2)}) copy-start(f32[2,15,4096]{2,1,0:T(8,128)} %slice.1007) | copy-start | bytes 1474564
  27.6 36.6 %copy-start.22 = (f32[2,16,4096]{2,1,0:T(8,128)}, f32[2,16,4096]{2,1,0:T(8,128)S(1)}, u32[]{:S(2)}) copy-start(f32[2,16,4096]{2,1,0:T(8,128)S(1)} %fusion.173) | copy-start | bytes 1572868
  30.8 18.8 %copy-start.13 = (f32[2,16,4096]{2,1,0:T(8,128)}, f32[2,16,4096]{2,1,0:T(8,128)S(1)}, u32[]{:S(2)}) copy-start(f32[2,16,4096]{2,1,0:T(8,128)S(1)} %fusion.170) | copy-start | bytes 1572868
  33.6 26.0 %collective-permute-start.5 = (f32[2,2,1024]{2,0,1:T(2,128)}, f32[2,2,1024]{2,0,1:T(2,128)}, u32[]{:S(2)}, u32[]{:S(2)}) collective-permute-start(f32[2,2,1024]{2,0,1:T(2,128)} %pad_maximum_fusion.19), channel_id=1, source_target_pairs={{0,1},{1,2},{2,3},{4,5},{5,6},{6,7},{8,9},{9,10},{10,11},{12,13},{... | collective-permute-start | bytes 49160 | tf_op jit(solution)/shard_map/ppermute | solution.py:18
  41.0 20.7 %collective-permute-start.6 = (f32[2,2,1,4096]{3,1,2,0:T(2,128)}, f32[2,2,1,4096]{3,1,2,0:T(2,128)}, u32[]{:S(2)}, u32[]{:S(2)}) collective-permute-start(f32[2,2,1,4096]{3,1,2,0:T(2,128)} %pad_maximum_fusion.2), channel_id=1, source_target_pairs={{0,4},{4,8},{8,12},{1,5},{5,9},{9,13},{2,6},{6,10},{10,14},{3,7},{... | collective-permute-start | bytes 196616 | tf_op jit(solution)/shard_map/ppermute | solution.py:18
  46.9 15.8 %copy-start.71 = (f32[2]{0:T(128)S(1)}, f32[2]{0:T(128)}, u32[]{:S(2)}) copy-start(f32[2]{0:T(128)} %get-tuple-element.9) | copy-start | bytes 28
  49.6 14.5 %copy-start.29 = (f32[2,16,4096]{2,1,0:T(8,128)}, f32[2,16,4096]{2,1,0:T(8,128)S(1)}, u32[]{:S(2)}) copy-start(f32[2,16,4096]{2,1,0:T(8,128)S(1)} %get-tuple-element.23) | copy-start | bytes 1572868
  49.6 14.5 %copy-start.37 = (f32[2,16,4096]{2,1,0:T(8,128)}, f32[2,16,4096]{2,1,0:T(8,128)S(1)}, u32[]{:S(2)}) copy-start(f32[2,16,4096]{2,1,0:T(8,128)S(1)} %get-tuple-element.22) | copy-start | bytes 1572868
  50.5 16.9 %collective-permute-start.18 = (f32[2,2,1,4096]{3,1,2,0:T(2,128)}, f32[2,2,1,4096]{3,1,2,0:T(2,128)}, u32[]{:S(2)}, u32[]{:S(2)}) collective-permute-start(f32[2,2,1,4096]{3,1,2,0:T(2,128)} %pad_maximum_fusion.8), channel_id=1, source_target_pairs={{0,4},{4,8},{8,12},{1,5},{5,9},{9,13},{2,6},{6,10},{10,14},{3,7},{... | collective-permute-start | bytes 196616 | tf_op jit(solution)/shard_map/ppermute | solution.py:18
  55.4 5.7 %collective-permute-start.2 = (f32[2,2,1024]{2,0,1:T(2,128)S(1)}, f32[2,2,1024]{2,0,1:T(2,128)S(1)}, u32[]{:S(2)}, u32[]{:S(2)}) collective-permute-start(f32[2,2,1024]{2,0,1:T(2,128)S(1)} %pad_maximum_fusion.17), channel_id=1, source_target_pairs={{0,1},{1,2},{2,3},{4,5},{5,6},{6,7},{8,9},{9,10},{10,11},{12,13},{... | collective-permute-start | bytes 49160 | tf_op jit(solution)/shard_map/ppermute | solution.py:18
  66.1 9.3 %collective-permute-start.8 = (f32[2,2,1024]{2,0,1:T(2,128)S(1)}, f32[2,2,1024]{2,0,1:T(2,128)S(1)}, u32[]{:S(2)}, u32[]{:S(2)}) collective-permute-start(f32[2,2,1024]{2,0,1:T(2,128)S(1)} %pad_maximum_fusion.20), channel_id=1, source_target_pairs={{1,0},{2,1},{3,2},{5,4},{6,5},{7,6},{9,8},{10,9},{11,10},{13,12},{... | collective-permute-start | bytes 49160 | tf_op jit(solution)/shard_map/ppermute | solution.py:18
  74.1 6.2 %collective-permute-start.7 = (f32[2,2,1,4096]{3,1,2,0:T(2,128)S(1)}, f32[2,2,1,4096]{3,1,2,0:T(2,128)S(1)}, u32[]{:S(2)}, u32[]{:S(2)}) collective-permute-start(f32[2,2,1,4096]{3,1,2,0:T(2,128)S(1)} %pad_maximum_fusion.3), channel_id=1, source_target_pairs={{4,0},{8,4},{12,8},{5,1},{9,5},{13,9},{6,2},{10,6},{14,10},{7,3},{... | collective-permute-start | bytes 196616 | tf_op jit(solution)/shard_map/ppermute | solution.py:18
  80.3 14.6 %copy-start.70 = (f32[2]{0:T(128)S(1)}, f32[2]{0:T(128)}, u32[]{:S(2)}) copy-start(f32[2]{0:T(128)} %get-tuple-element.8) | copy-start | bytes 28
  84.1 8.9 %collective-permute-start.9 = (f32[2,2,1024]{2,0,1:T(2,128)S(1)}, f32[2,2,1024]{2,0,1:T(2,128)S(1)}, u32[]{:S(2)}, u32[]{:S(2)}) collective-permute-start(f32[2,2,1024]{2,0,1:T(2,128)S(1)} %pad_maximum_fusion.21), channel_id=1, source_target_pairs={{0,1},{1,2},{2,3},{4,5},{5,6},{6,7},{8,9},{9,10},{10,11},{12,13},{... | collective-permute-start | bytes 49160 | tf_op jit(solution)/shard_map/ppermute | solution.py:18
  89.0 5.8 %collective-permute-start.10 = (f32[2,2,1,4096]{3,1,2,0:T(2,128)S(1)}, f32[2,2,1,4096]{3,1,2,0:T(2,128)S(1)}, u32[]{:S(2)}, u32[]{:S(2)}) collective-permute-start(f32[2,2,1,4096]{3,1,2,0:T(2,128)S(1)} %pad_maximum_fusion.4), channel_id=1, source_target_pairs={{0,4},{4,8},{8,12},{1,5},{5,9},{9,13},{2,6},{6,10},{10,14},{3,7},{... | collective-permute-start | bytes 196616 | tf_op jit(solution)/shard_map/ppermute | solution.py:18
  98.4 21.3 %copy-start.1 = (f32[2,16,4096]{2,1,0:T(8,128)}, f32[2,16,4096]{2,1,0:T(8,128)S(1)}, u32[]{:S(2)}) copy-start(f32[2,16,4096]{2,1,0:T(8,128)S(1)} %get-tuple-element.36) | copy-start | bytes 1572868
  102.5 6.3 %copy-start.6 = (f32[2,16,4096]{2,1,0:T(8,128)S(1)}, f32[2,16,4096]{2,1,0:T(8,128)}, u32[]{:S(2)}) copy-start(f32[2,16,4096]{2,1,0:T(8,128)} %get-tuple-element.37) | copy-start | bytes 1572868
  103.3 9.8 %collective-permute-start.12 = (f32[2,2,1024]{2,0,1:T(2,128)S(1)}, f32[2,2,1024]{2,0,1:T(2,128)}, u32[]{:S(2)}, u32[]{:S(2)}) collective-permute-start(f32[2,2,1024]{2,0,1:T(2,128)S(1)} %pad_maximum_fusion.22), channel_id=1, source_target_pairs={{1,0},{2,1},{3,2},{5,4},{6,5},{7,6},{9,8},{10,9},{11,10},{13,12},{... | collective-permute-start | bytes 49160 | tf_op jit(solution)/shard_map/ppermute | solution.py:18
  111.8 6.8 %collective-permute-start.11 = (f32[2,2,1,4096]{3,1,2,0:T(2,128)}, f32[2,2,1,4096]{3,1,2,0:T(2,128)}, u32[]{:S(2)}, u32[]{:S(2)}) collective-permute-start(f32[2,2,1,4096]{3,1,2,0:T(2,128)} %pad_maximum_fusion.5), channel_id=1, source_target_pairs={{4,0},{8,4},{12,8},{5,1},{9,5},{13,9},{6,2},{10,6},{14,10},{7,3},{... | collective-permute-start | bytes 196616 | tf_op jit(solution)/shard_map/ppermute | solution.py:18
  119.6 17.3 %copy-start.65 = (s32[2]{0:T(128)S(1)}, s32[2]{0:T(128)}, u32[]{:S(2)}) copy-start(s32[2]{0:T(128)} %copy-done.64) | copy-start | bytes 28
  119.7 17.3 %copy-start.69 = (f32[2]{0:T(128)S(1)}, f32[2]{0:T(128)}, u32[]{:S(2)}) copy-start(f32[2]{0:T(128)} %get-tuple-element.10) | copy-start | bytes 28
  124.5 10.4 %collective-permute-start.13 = (f32[2,2,1024]{2,0,1:T(2,128)S(1)}, f32[2,2,1024]{2,0,1:T(2,128)S(1)}, u32[]{:S(2)}, u32[]{:S(2)}) collective-permute-start(f32[2,2,1024]{2,0,1:T(2,128)S(1)} %pad_maximum_fusion.23), channel_id=1, source_target_pairs={{0,1},{1,2},{2,3},{4,5},{5,6},{6,7},{8,9},{9,10},{10,11},{12,13},{... | collective-permute-start | bytes 49160 | tf_op jit(solution)/shard_map/ppermute | solution.py:18
  131.0 5.8 %collective-permute-start.14 = (f32[2,2,1,4096]{3,1,2,0:T(2,128)S(1)}, f32[2,2,1,4096]{3,1,2,0:T(2,128)S(1)}, u32[]{:S(2)}, u32[]{:S(2)}) collective-permute-start(f32[2,2,1,4096]{3,1,2,0:T(2,128)S(1)} %pad_maximum_fusion.6), channel_id=1, source_target_pairs={{0,4},{4,8},{8,12},{1,5},{5,9},{9,13},{2,6},{6,10},{10,14},{3,7},{... | collective-permute-start | bytes 196616 | tf_op jit(solution)/shard_map/ppermute | solution.py:18
  145.8 6.4 %copy-start.5 = (f32[2,16,4096]{2,1,0:T(8,128)S(1)}, f32[2,16,4096]{2,1,0:T(8,128)}, u32[]{:S(2)}) copy-start(f32[2,16,4096]{2,1,0:T(8,128)} %get-tuple-element.35) | copy-start | bytes 1572868
  146.6 10.0 %collective-permute-start.16 = (f32[2,2,1024]{2,0,1:T(2,128)S(1)}, f32[2,2,1024]{2,0,1:T(2,128)}, u32[]{:S(2)}, u32[]{:S(2)}) collective-permute-start(f32[2,2,1024]{2,0,1:T(2,128)S(1)} %pad_maximum_fusion.24), channel_id=1, source_target_pairs={{1,0},{2,1},{3,2},{5,4},{6,5},{7,6},{9,8},{10,9},{11,10},{13,12},{... | collective-permute-start | bytes 49160 | tf_op jit(solution)/shard_map/ppermute | solution.py:18
  155.3 6.8 %collective-permute-start.15 = (f32[2,2,1,4096]{3,1,2,0:T(2,128)}, f32[2,2,1,4096]{3,1,2,0:T(2,128)}, u32[]{:S(2)}, u32[]{:S(2)}) collective-permute-start(f32[2,2,1,4096]{3,1,2,0:T(2,128)} %pad_maximum_fusion.7), channel_id=1, source_target_pairs={{4,0},{8,4},{12,8},{5,1},{9,5},{13,9},{6,2},{10,6},{14,10},{7,3},{... | collective-permute-start | bytes 196616 | tf_op jit(solution)/shard_map/ppermute | solution.py:18
  171.8 12.0 %collective-permute-start.17 = (f32[2,2,1024]{2,0,1:T(2,128)S(1)}, f32[2,2,1024]{2,0,1:T(2,128)}, u32[]{:S(2)}, u32[]{:S(2)}) collective-permute-start(f32[2,2,1024]{2,0,1:T(2,128)S(1)} %pad_maximum_fusion.25), channel_id=1, source_target_pairs={{0,1},{1,2},{2,3},{4,5},{5,6},{6,7},{8,9},{9,10},{10,11},{12,13},{... | collective-permute-start | bytes 49160 | tf_op jit(solution)/shard_map/ppermute | solution.py:18
  179.3 6.1 %collective-permute-start.19 = (f32[2,2,1,4096]{3,1,2,0:T(2,128)}, f32[2,2,1,4096]{3,1,2,0:T(2,128)}, u32[]{:S(2)}, u32[]{:S(2)}) collective-permute-start(f32[2,2,1,4096]{3,1,2,0:T(2,128)} %pad_maximum_fusion.9), channel_id=1, source_target_pairs={{0,4},{4,8},{8,12},{1,5},{5,9},{9,13},{2,6},{6,10},{10,14},{3,7},{... | collective-permute-start | bytes 196616 | tf_op jit(solution)/shard_map/ppermute | solution.py:18
  194.1 8.1 %copy-start.34 = (f32[2,16,4096]{2,1,0:T(8,128)S(1)}, f32[2,16,4096]{2,1,0:T(8,128)}, u32[]{:S(2)}) copy-start(f32[2,16,4096]{2,1,0:T(8,128)} %copy-done.33) | copy-start | bytes 1572868
  194.1 9.1 %copy-start.42 = (f32[2,16,4096]{2,1,0:T(8,128)S(1)}, f32[2,16,4096]{2,1,0:T(8,128)}, u32[]{:S(2)}) copy-start(f32[2,16,4096]{2,1,0:T(8,128)} %copy-done.41) | copy-start | bytes 1572868
  194.1 10.2 %copy-start.21 = (f32[2,16,4096]{2,1,0:T(8,128)S(1)}, f32[2,16,4096]{2,1,0:T(8,128)}, u32[]{:S(2)}) copy-start(f32[2,16,4096]{2,1,0:T(8,128)} %copy-done.20) | copy-start | bytes 1572868
  194.1 12.3 %collective-permute-start.21 = (f32[2,2,1024]{2,0,1:T(2,128)S(1)}, f32[2,2,1024]{2,0,1:T(2,128)}, u32[]{:S(2)}, u32[]{:S(2)}) collective-permute-start(f32[2,2,1024]{2,0,1:T(2,128)S(1)} %pad_maximum_fusion.26), channel_id=1, source_target_pairs={{1,0},{2,1},{3,2},{5,4},{6,5},{7,6},{9,8},{10,9},{11,10},{13,12},{... | collective-permute-start | bytes 49160 | tf_op jit(solution)/shard_map/ppermute | solution.py:18
  205.1 6.7 %collective-permute-start.20 = (f32[2,2,1,4096]{3,1,2,0:T(2,128)}, f32[2,2,1,4096]{3,1,2,0:T(2,128)S(1)}, u32[]{:S(2)}, u32[]{:S(2)}) collective-permute-start(f32[2,2,1,4096]{3,1,2,0:T(2,128)} %pad_maximum_fusion.10), channel_id=1, source_target_pairs={{4,0},{8,4},{12,8},{5,1},{9,5},{13,9},{6,2},{10,6},{14,10},{7,3},{... | collective-permute-start | bytes 196616 | tf_op jit(solution)/shard_map/ppermute | solution.py:18
  217.2 11.1 %collective-permute-start.22 = (f32[2,2,1024]{2,0,1:T(2,128)S(1)}, f32[2,2,1024]{2,0,1:T(2,128)}, u32[]{:S(2)}, u32[]{:S(2)}) collective-permute-start(f32[2,2,1024]{2,0,1:T(2,128)S(1)} %pad_maximum_fusion.27), channel_id=1, source_target_pairs={{0,1},{1,2},{2,3},{4,5},{5,6},{6,7},{8,9},{9,10},{10,11},{12,13},{... | collective-permute-start | bytes 49160 | tf_op jit(solution)/shard_map/ppermute | solution.py:18
  224.3 6.1 %collective-permute-start.23 = (f32[2,2,1,4096]{3,1,2,0:T(2,128)}, f32[2,2,1,4096]{3,1,2,0:T(2,128)S(1)}, u32[]{:S(2)}, u32[]{:S(2)}) collective-permute-start(f32[2,2,1,4096]{3,1,2,0:T(2,128)} %pad_maximum_fusion.11), channel_id=1, source_target_pairs={{0,4},{4,8},{8,12},{1,5},{5,9},{9,13},{2,6},{6,10},{10,14},{3,7},{... | collective-permute-start | bytes 196616 | tf_op jit(solution)/shard_map/ppermute | solution.py:18
  234.9 8.1 %copy-start.45 = (f32[2,16,4096]{2,1,0:T(8,128)S(1)}, f32[2,16,4096]{2,1,0:T(8,128)}, u32[]{:S(2)}) copy-start(f32[2,16,4096]{2,1,0:T(8,128)} %copy-done.44) | copy-start | bytes 1572868
  234.9 9.2 %copy-start.19 = (f32[2,16,4096]{2,1,0:T(8,128)S(1)}, f32[2,16,4096]{2,1,0:T(8,128)}, u32[]{:S(2)}) copy-start(f32[2,16,4096]{2,1,0:T(8,128)} %copy-done.18) | copy-start | bytes 1572868
  234.9 12.3 %collective-permute-start.25 = (f32[2,2,1024]{2,0,1:T(2,128)S(1)}, f32[2,2,1024]{2,0,1:T(2,128)}, u32[]{:S(2)}, u32[]{:S(2)}) collective-permute-start(f32[2,2,1024]{2,0,1:T(2,128)S(1)} %pad_maximum_fusion.28), channel_id=1, source_target_pairs={{1,0},{2,1},{3,2},{5,4},{6,5},{7,6},{9,8},{10,9},{11,10},{13,12},{... | collective-permute-start | bytes 49160 | tf_op jit(solution)/shard_map/ppermute | solution.py:18
  246.0 6.6 %collective-permute-start.24 = (f32[2,2,1,4096]{3,1,2,0:T(2,128)}, f32[2,2,1,4096]{3,1,2,0:T(2,128)S(1)}, u32[]{:S(2)}, u32[]{:S(2)}) collective-permute-start(f32[2,2,1,4096]{3,1,2,0:T(2,128)} %pad_maximum_fusion.12), channel_id=1, source_target_pairs={{4,0},{8,4},{12,8},{5,1},{9,5},{13,9},{6,2},{10,6},{14,10},{7,3},{... | collective-permute-start | bytes 196616 | tf_op jit(solution)/shard_map/ppermute | solution.py:18
  258.0 11.1 %collective-permute-start.26 = (f32[2,2,1024]{2,0,1:T(2,128)S(1)}, f32[2,2,1024]{2,0,1:T(2,128)}, u32[]{:S(2)}, u32[]{:S(2)}) collective-permute-start(f32[2,2,1024]{2,0,1:T(2,128)S(1)} %pad_maximum_fusion.29), channel_id=1, source_target_pairs={{0,1},{1,2},{2,3},{4,5},{5,6},{6,7},{8,9},{9,10},{10,11},{12,13},{... | collective-permute-start | bytes 49160 | tf_op jit(solution)/shard_map/ppermute | solution.py:18
  265.1 6.1 %collective-permute-start.27 = (f32[2,2,1,4096]{3,1,2,0:T(2,128)}, f32[2,2,1,4096]{3,1,2,0:T(2,128)S(1)}, u32[]{:S(2)}, u32[]{:S(2)}) collective-permute-start(f32[2,2,1,4096]{3,1,2,0:T(2,128)} %pad_maximum_fusion.13), channel_id=1, source_target_pairs={{0,4},{4,8},{8,12},{1,5},{5,9},{9,13},{2,6},{6,10},{10,14},{3,7},{... | collective-permute-start | bytes 196616 | tf_op jit(solution)/shard_map/ppermute | solution.py:18
  277.5 10.1 %copy-start.17 = (f32[2,16,4096]{2,1,0:T(8,128)S(1)}, f32[2,16,4096]{2,1,0:T(8,128)}, u32[]{:S(2)}) copy-start(f32[2,16,4096]{2,1,0:T(8,128)} %copy-done.16) | copy-start | bytes 1572868
  278.0 7.6 %copy-start.32 = (f32[2,16,4096]{2,1,0:T(8,128)S(1)}, f32[2,16,4096]{2,1,0:T(8,128)}, u32[]{:S(2)}) copy-start(f32[2,16,4096]{2,1,0:T(8,128)} %copy-done.31) | copy-start | bytes 1572868
  278.0 8.6 %copy-start.40 = (f32[2,16,4096]{2,1,0:T(8,128)S(1)}, f32[2,16,4096]{2,1,0:T(8,128)}, u32[]{:S(2)}) copy-start(f32[2,16,4096]{2,1,0:T(8,128)} %copy-done.39) | copy-start | bytes 1572868
  278.0 11.7 %collective-permute-start.29 = (f32[2,2,1024]{2,0,1:T(2,128)S(1)}, f32[2,2,1024]{2,0,1:T(2,128)}, u32[]{:S(2)}, u32[]{:S(2)}) collective-permute-start(f32[2,2,1024]{2,0,1:T(2,128)S(1)} %pad_maximum_fusion.30), channel_id=1, source_target_pairs={{1,0},{2,1},{3,2},{5,4},{6,5},{7,6},{9,8},{10,9},{11,10},{13,12},{... | collective-permute-start | bytes 49160 | tf_op jit(solution)/shard_map/ppermute | solution.py:18
  279.5 16.4 %copy-start.15 = (f32[2,16,4096]{2,1,0:T(8,128)S(1)}, f32[2,16,4096]{2,1,0:T(8,128)}, u32[]{:S(2)}) copy-start(f32[2,16,4096]{2,1,0:T(8,128)} %copy-done.14) | copy-start | bytes 1572868
  279.5 16.4 %copy-start.30 = (f32[2,16,4096]{2,1,0:T(8,128)S(1)}, f32[2,16,4096]{2,1,0:T(8,128)}, u32[]{:S(2)}) copy-start(f32[2,16,4096]{2,1,0:T(8,128)} %get-tuple-element.42) | copy-start | bytes 1572868
  288.4 6.5 %collective-permute-start.28 = (f32[2,2,1,4096]{3,1,2,0:T(2,128)S(1)}, f32[2,2,1,4096]{3,1,2,0:T(2,128)}, u32[]{:S(2)}, u32[]{:S(2)}) collective-permute-start(f32[2,2,1,4096]{3,1,2,0:T(2,128)S(1)} %pad_maximum_fusion.14), channel_id=1, source_target_pairs={{4,0},{8,4},{12,8},{5,1},{9,5},{13,9},{6,2},{10,6},{14,10},{7,3},{... | collective-permute-start | bytes 196616 | tf_op jit(solution)/shard_map/ppermute | solution.py:18
  300.1 9.1 %collective-permute-start.30 = (f32[2,2,1024]{2,0,1:T(2,128)S(1)}, f32[2,2,1024]{2,0,1:T(2,128)S(1)}, u32[]{:S(2)}, u32[]{:S(2)}) collective-permute-start(f32[2,2,1024]{2,0,1:T(2,128)S(1)} %pad_maximum_fusion.31), channel_id=1, source_target_pairs={{0,1},{1,2},{2,3},{4,5},{5,6},{6,7},{8,9},{9,10},{10,11},{12,13},{... | collective-permute-start | bytes 49160 | tf_op jit(solution)/shard_map/ppermute | solution.py:18
  305.0 5.8 %collective-permute-start.31 = (f32[2,2,1,4096]{3,1,2,0:T(2,128)S(1)}, f32[2,2,1,4096]{3,1,2,0:T(2,128)S(1)}, u32[]{:S(2)}, u32[]{:S(2)}) collective-permute-start(f32[2,2,1,4096]{3,1,2,0:T(2,128)S(1)} %pad_maximum_fusion.15), channel_id=1, source_target_pairs={{0,4},{4,8},{8,12},{1,5},{5,9},{9,13},{2,6},{6,10},{10,14},{3,7},{... | collective-permute-start | bytes 196616 | tf_op jit(solution)/shard_map/ppermute | solution.py:18
  321.8 15.4 %copy-start.72 = (s32[1,64]{1,0:T(1,128)S(1)}, s32[1,64]{1,0:T(1,128)}, u32[]{:S(2)}) copy-start(s32[1,64]{1,0:T(1,128)} %param.15) | copy-start | bytes 772
  333.0 10.3 %all-to-all-start.1 = ((f32[4,16,2,512]{3,1,2,0:T(8,128)}), f32[4,16,2,512]{3,1,2,0:T(8,128)S(1)}, u32[]{:S(2)}, u32[]{:S(2)}) async-start(f32[4,16,2,512]{3,1,2,0:T(8,128)} %copy.86), calls=%async_computation.1 | async-start | bytes 524288 | tf_op jit(solution)/shard_map/all_to_all | solution.py:174
  (42 other events, 109.7 us)
where the time goes:
time: 349 us; the launch traced here: 345 us
  local copies, waits for them, and re-layouts  122 us (35%)
  starting transfers between devices  102 us (29%)
  other arithmetic  71.6 us (21%)
  waiting for transfers between devices  43 us (12%)
  blocking collectives  3.94 us (1%)
    ppermute x32, starting transfers between devices, passed_along(): return lax.ppermute(shard, axis, pairs)  98.3 us
    ppermute x32, waiting for transfers between devices, passed_along(): return lax.ppermute(shard, axis, pairs)  36.9 us
    sub x8, other arithmetic, magnetic_update(): magnetic[0]  23.2 us
    slice x16, local copies, waits for them, and re-layouts, upper_y(): return jnp.concatenate([values[..., z_cells:], ghosts], axis=-1)  21.3 us
    slice x16, local copies, waits for them, and re-layouts, upper_z(): values[..., 1:]  17.2 us
    reduce_sum x3, other arithmetic, per_device(): density = density + jnp.sum(intersection, axis=0)  16 us
    slice x16, local copies, waits for them, and re-layouts, upper_x(): return jnp.concatenate([values[..., 1:, :], ghosts], axis=-2)  15.9 us
    unnamed x148, local copies, waits for them, and re-layouts  15 us
  transfers between devices with their start and end apart: 33, of which 14 were waited for; matrix products, arithmetic and copies ran while one was open for 27% of the time, Pallas kernels for 0%

commit v1 on v0

v1 whole, which is shorter than its diff:
```python
import functools

import jax
import jax.numpy as jnp
from jax import lax
from jax.experimental import pallas as pl
from jax.experimental.pallas import tpu as pltpu
from jax.sharding import PartitionSpec as P

NZ = 64
STEPS = 4
BX = 4
BY = 4
COURANT = 0.55
MESH = pl.DeviceIdType.MESH


def split3(v):
    hi = v.astype(jnp.bfloat16)
    rest = v - hi.astype(jnp.float32)
    mid = rest.astype(jnp.bfloat16)
    low = (rest - mid.astype(jnp.float32)).astype(jnp.bfloat16)
    return jnp.concatenate([hi, mid, low], axis=0)


def kernel(
    n_gx, n_gy, cap,
    fwd, adj, perm, wave, cell, owner, slot, rows, out,
    E, H, fac, inc, asv, D, SE, SH, GE, GH, B, RB, S2, R2, RF, OH1, OH2,
    load_sem, perm_sem,
    exs, exr, hxs, hxr, eys, eyr, hys, hyr, src_sem, rt_s, rt_r,
):
    T = fac.shape[0]
    X = fac.shape[1]
    NS = fwd.shape[0]
    NB = out.shape[0]
    sims = 2 * NS
    src = lax.axis_index("src")
    gx = lax.axis_index("gx")
    gy = lax.axis_index("gy")

    loads = {}
    for sim in range(sims):
        state = fwd if sim < NS else adj
        s = sim % NS
        for xt in range(X // 8):
            loads[sim, 0, xt] = pltpu.make_async_copy(
                state.at[s, pl.ds(0, 3), xt],
                E.at[sim, :, pl.ds(0, T), pl.ds(8 * xt, 8), :],
                load_sem.at[sim, 0, xt],
            )
            loads[sim, 1, xt] = pltpu.make_async_copy(
                state.at[s, pl.ds(3, 3), xt],
                H.at[sim, :, pl.ds(1, T), pl.ds(8 + 8 * xt, 8), :],
                load_sem.at[sim, 1, xt],
            )
    perms = [
        pltpu.make_async_copy(
            perm.at[xt], fac.at[:, pl.ds(8 * xt, 8), :], perm_sem.at[xt]
        )
        for xt in range(X // 8)
    ]
    for sim in range(sims):
        for xt in range(X // 8):
            loads[sim, 0, xt].start()
    for sim in range(sims):
        for xt in range(X // 8):
            loads[sim, 1, xt].start()
    for c in perms:
        c.start()

    zero_tile = jnp.zeros((X, 128), jnp.float32)
    zero_row = jnp.zeros((1, 128), jnp.float32)
    for sim in range(sims):
        for c in (0, 2):
            E[sim, c, T, 0:X, :] = zero_tile
            H[sim, c, 0, 8 : 8 + X, :] = zero_tile

    def zero_ghosts(t, carry):
        for sim in range(sims):
            for c in (1, 2):
                E[sim, c, t, X : X + 1, :] = zero_row
                H[sim, c, t + 1, 7:8, :] = zero_row
        return carry

    lax.fori_loop(0, T, zero_ghosts, 0)

    barrier = pltpu.get_barrier_semaphore()
    partners = [
        {"gx": lax.rem(gx + 1, n_gx)},
        {"gx": lax.rem(gx + n_gx - 1, n_gx)},
        {"src": 1 - src},
    ]
    for d in range(1, n_gy):
        partners.append({"gy": lax.rem(gy + d, n_gy)})
    for device in partners:
        pl.semaphore_signal(barrier, inc=1, device_id=device, device_id_type=MESH)

    KB = 3 * NB
    LBY = owner.shape[1]
    dest = jnp.where(owner[...] >= 0, owner[...] * cap + slot[...], -1)
    dest = dest.astype(jnp.float32)
    q_i = lax.broadcasted_iota(jnp.int32, (LBY, KB), 0)
    b_i = lax.broadcasted_iota(jnp.int32, (LBY, KB), 1)
    pick = jnp.where(b_i % LBY == q_i, 1.0, 0.0)
    wide = jnp.dot(dest, pick, preferred_element_type=jnp.float32)
    p_i = lax.broadcasted_iota(jnp.int32, wide.shape, 0)
    l_i = lax.broadcasted_iota(jnp.int32, wide.shape, 1)
    line = jnp.sum(
        jnp.where((l_i % NB) // LBY == p_i, wide, 0.0), axis=0, keepdims=True
    )
    r_f = lax.broadcasted_iota(jnp.int32, (NB, KB), 0).astype(jnp.float32)
    OH1[...] = jnp.where(line == r_f, 1.0, 0.0).astype(jnp.bfloat16)
    m_i = lax.broadcasted_iota(jnp.int32, (NB, KB), 0)
    k_i = lax.broadcasted_iota(jnp.int32, (NB, KB), 1)
    pick = jnp.where(k_i % NB == m_i, 1.0, 0.0)
    row8 = jnp.broadcast_to(rows[...].astype(jnp.float32), (8, NB))
    line = jnp.dot(row8, pick, preferred_element_type=jnp.float32)[0:1, :]
    OH2[...] = jnp.where(line == r_f, 1.0, 0.0).astype(jnp.bfloat16)

    def e_copies(sim):
        x = pltpu.make_async_remote_copy(
            SE.at[sim], GE.at[sim], exs.at[sim], exr.at[sim],
            device_id={"gx": gx - 1}, device_id_type=MESH,
        )
        ys = [
            pltpu.make_async_remote_copy(
                E.at[sim, c, 0, pl.ds(0, X), :],
                E.at[sim, c, T, pl.ds(0, X), :],
                eys.at[sim, i], eyr.at[sim, i],
                device_id={"gy": gy - 1}, device_id_type=MESH,
            )
            for i, c in enumerate((0, 2))
        ]
        return x, ys

    def h_copies(sim):
        x = pltpu.make_async_remote_copy(
            SH.at[sim], GH.at[sim], hxs.at[sim], hxr.at[sim],
            device_id={"gx": gx + 1}, device_id_type=MESH,
        )
        ys = [
            pltpu.make_async_remote_copy(
                H.at[sim, c, T, pl.ds(8, X), :],
                H.at[sim, c, 0, pl.ds(8, X), :],
                hys.at[sim, i], hyr.at[sim, i],
                device_id={"gy": gy + 1}, device_id_type=MESH,
            )
            for i, c in enumerate((0, 2))
        ]
        return x, ys

    def e_send(sim):
        x, ys = e_copies(sim)

        @pl.when(gx > 0)
        def _():
            x.start()

        @pl.when(gy > 0)
        def _():
            for y in ys:
                y.start()

    def e_sent(sim):
        x, ys = e_copies(sim)

        @pl.when(gx > 0)
        def _():
            x.wait_send()

        @pl.when(gy > 0)
        def _():
            for y in ys:
                y.wait_send()

    def h_send(sim):
        x, ys = h_copies(sim)

        @pl.when(gx < n_gx - 1)
        def _():
            x.start()

        @pl.when(gy < n_gy - 1)
        def _():
            for y in ys:
                y.start()

    def h_sent(sim):
        x, ys = h_copies(sim)

        @pl.when(gx < n_gx - 1)
        def _():
            x.wait_send()

        @pl.when(gy < n_gy - 1)
        def _():
            for y in ys:
                y.wait_send()

    def e_arrive(sim):
        x, ys = e_copies(sim)

        @pl.when(gx < n_gx - 1)
        def _():
            x.wait_recv()

            def unpack(t, carry):
                E[sim, 1, t, X : X + 1, :] = GE[sim, 0, t]
                E[sim, 2, t, X : X + 1, :] = GE[sim, 1, t]
                return carry

            lax.fori_loop(0, T, unpack, 0, unroll=8)

        @pl.when(gy < n_gy - 1)
        def _():
            for y in ys:
                y.wait_recv()

    def h_arrive(sim):
        x, ys = h_copies(sim)

        @pl.when(gx > 0)
        def _():
            x.wait_recv()

            def unpack(t, carry):
                H[sim, 1, t + 1, 7:8, :] = GH[sim, 0, t]
                H[sim, 2, t + 1, 7:8, :] = GH[sim, 1, t]
                return carry

            lax.fori_loop(0, T, unpack, 0, unroll=8)

        @pl.when(gy > 0)
        def _():
            for y in ys:
                y.wait_recv()

    lane = lax.broadcasted_iota(jnp.int32, (X, 128), 1)
    row = lax.broadcasted_iota(jnp.int32, (X, 128), 0)
    z = lane % NZ
    z_first = z == 0
    z_last = z == NZ - 1
    low = lane < NZ
    cells_yz = T * 128
    linear = row * cells_yz + lane

    def h_phase(sim):
        def tile(t):
            ex = E[sim, 0, t, 0:X, :]
            ey = E[sim, 1, t, 0:X, :]
            ez = E[sim, 2, t, 0:X, :]
            exn = E[sim, 0, t + 1, 0:X, :]
            ezn = E[sim, 2, t + 1, 0:X, :]
            eyx = E[sim, 1, t, 1 : X + 1, :]
            ezx = E[sim, 2, t, 1 : X + 1, :]
            exy = pltpu.roll(jnp.where(low, exn, ex), NZ, 1)
            ezy = pltpu.roll(jnp.where(low, ezn, ez), NZ, 1)
            exz = jnp.where(z_last, 0.0, pltpu.roll(ex, 127, 1))
            eyz = jnp.where(z_last, 0.0, pltpu.roll(ey, 127, 1))
            hx = H[sim, 0, t + 1, 8 : 8 + X, :]
            hy = H[sim, 1, t + 1, 8 : 8 + X, :]
            hz = H[sim, 2, t + 1, 8 : 8 + X, :]
            hx = hx - COURANT * ((ezy - ez) - (eyz - ey))
            hy = hy - COURANT * ((exz - ex) - (ezx - ez))
            hz = hz - COURANT * ((eyx - ey) - (exy - ex))
            H[sim, 0, t + 1, 8 : 8 + X, :] = hx
            H[sim, 1, t + 1, 8 : 8 + X, :] = hy
            H[sim, 2, t + 1, 8 : 8 + X, :] = hz
            SH[sim, 0, t] = hy[X - 1 : X, :]
            SH[sim, 1, t] = hz[X - 1 : X, :]

        def body(i, carry):
            tile(2 * i)
            tile(2 * i + 1)
            return carry

        lax.fori_loop(0, T // 2, body, 0)

    def e_phase(sim, step):
        s = sim % NS
        forward = sim < NS
        if forward:
            lx = cell[s, 0] - gx * X
            lyz = (cell[s, 1] - gy * (cells_yz // NZ)) * NZ + cell[s, 2]
            inside = (lx >= 0) & (lx < X) & (lyz >= 0) & (lyz < cells_yz)
            target = jnp.where(inside, lx * cells_yz + lyz, -1)
            pulse = wave[s, step]

        def tile(t):
            hx = H[sim, 0, t + 1, 8 : 8 + X, :]
            hy = H[sim, 1, t + 1, 8 : 8 + X, :]
            hz = H[sim, 2, t + 1, 8 : 8 + X, :]
            hxp = H[sim, 0, t, 8 : 8 + X, :]
            hzp = H[sim, 2, t, 8 : 8 + X, :]
            hyx = H[sim, 1, t + 1, 7 : 7 + X, :]
            hzx = H[sim, 2, t + 1, 7 : 7 + X, :]
            hxy = pltpu.roll(jnp.where(low, hx, hxp), NZ, 1)
            hzy = pltpu.roll(jnp.where(low, hz, hzp), NZ, 1)
            hxz = jnp.where(z_first, 0.0, pltpu.roll(hx, 1, 1))
            hyz = jnp.where(z_first, 0.0, pltpu.roll(hy, 1, 1))
            f = fac[t]
            d0 = f * ((hz - hzy) - (hy - hyz))
            d1 = f * ((hx - hxz) - (hz - hzx))
            d2 = f * ((hy - hyx) - (hx - hxy))
            if forward:
                hit = linear == target - t * 128
                d2 = d2 + jnp.where(hit, pulse, 0.0)
            if not (forward and step == STEPS - 1):
                e0 = E[sim, 0, t, 0:X, :] + d0
                e1 = E[sim, 1, t, 0:X, :] + d1
                e2 = E[sim, 2, t, 0:X, :] + d2
            if step < STEPS - 1:
                E[sim, 0, t, 0:X, :] = e0
                E[sim, 1, t, 0:X, :] = e1
                E[sim, 2, t, 0:X, :] = e2
                SE[sim, 0, t] = e1[0:1, :]
                SE[sim, 1, t] = e2[0:1, :]
            if forward:
                if step < 2:
                    inc[s, step, 0, t] = d0
                    inc[s, step, 1, t] = d1
                    inc[s, step, 2, t] = d2
                else:
                    if step == 2:
                        a = [E[NS + s, c, t, 0:X, :] for c in range(3)]
                    else:
                        a = [asv[s, c, t] for c in range(3)]
                    term = d0 * a[0] + d1 * a[1] + d2 * a[2]
                    if step == 2 and s == 0:
                        D[t] = term
                    else:
                        D[t] = D[t] + term
            else:
                if step == 0:
                    asv[s, 0, t] = e0
                    asv[s, 1, t] = e1
                    asv[s, 2, t] = e2
                elif step >= 2:
                    k = STEPS - 1 - step
                    total = D[t] + (
                        e0 * inc[s, k, 0, t] + e1 * inc[s, k, 1, t] + e2 * inc[s, k, 2, t]
                    )
                    if step == STEPS - 1 and s == NS - 1:
                        total = total * (f * (-1.0 / COURANT))
                    D[t] = total

        def body(i, carry):
            tile(2 * i)
            tile(2 * i + 1)
            return carry

        lax.fori_loop(0, T // 2, body, 0)

    pl.semaphore_wait(barrier, len(partners))
    for sim in range(sims):
        for xt in range(X // 8):
            loads[sim, 0, xt].wait()

        def pack(t, carry):
            SE[sim, 0, t] = E[sim, 1, t, 0:1, :]
            SE[sim, 1, t] = E[sim, 2, t, 0:1, :]
            return carry

        lax.fori_loop(0, T, pack, 0, unroll=8)
        e_send(sim)

    for c in perms:
        c.wait()

    def make_factor(t, carry):
        fac[t] = COURANT / fac[t]
        return carry

    lax.fori_loop(0, T, make_factor, 0)

    for step in range(STEPS):
        for sim in range(sims):
            if step == 0:
                for xt in range(X // 8):
                    loads[sim, 1, xt].wait()
            e_arrive(sim)
            if step > 0:
                h_sent(sim)
            h_phase(sim)
            h_send(sim)
        for sim in range(sims):
            h_arrive(sim)
            e_sent(sim)
            e_phase(sim, step)
            if step < STEPS - 1:
                e_send(sim)
    for sim in range(sims):
        h_sent(sim)

    half = BX // 2
    for h in range(2):
        for p in range(X // BX):
            for xi in range(half):
                for yh in range(BY // 2):
                    j = xi * (BY // 2) + yh
                    start = yh * X + BX * p + half * h + xi
                    B[h, p * LBY : (p + 1) * LBY, j * 128 : (j + 1) * 128] = D.reshape(
                        T * X, 128
                    )[pl.ds(start, LBY, stride=2 * X), :]
    peer = pltpu.make_async_remote_copy(
        B.at[1 - src], RB, src_sem.at[0], src_sem.at[1],
        device_id={"src": 1 - src}, device_id_type=MESH,
    )
    peer.start()
    peer.wait_recv()
    mine = B[src] + RB[...]
    routed = jnp.dot(OH1[...], split3(mine), preferred_element_type=jnp.float32)
    for o in range(n_gy):
        S2[o] = routed[o * cap : (o + 1) * cap, :]
    sends = []
    for d in range(1, n_gy):
        o = lax.rem(gy + d, n_gy)
        sends.append(
            pltpu.make_async_remote_copy(
                S2.at[o], R2.at[gy], rt_s.at[d], rt_r.at[d],
                device_id={"gy": o}, device_id_type=MESH,
            )
        )
        sends[-1].start()
    R2[gy] = S2[gy]
    for c in sends:
        c.wait_recv()
    for o in range(n_gy):
        RF[o * cap : (o + 1) * cap, :] = R2[o]
    out[...] = jnp.dot(OH2[...], split3(RF[...]), preferred_element_type=jnp.float32)
    for c in sends:
        c.wait_send()
    peer.wait_send()


def tiled(state):
    lead = state.shape[:-2]
    x, yz = state.shape[-2:]
    n = len(lead)
    state = state.reshape(lead + (x // 8, 8, yz // 128, 128))
    return state.transpose(tuple(range(n)) + (n, n + 2, n + 1, n + 3))


def per_device(
    n_gx, n_gy, forward_state, adjoint_state, permittivity, waveform, source_cell,
    block_owner, block_slot, owner_rows,
):
    NS = forward_state.shape[0]
    X, YZ = permittivity.shape
    T = YZ // 128
    NB = block_owner.shape[0] * block_owner.shape[1]
    cap = max(2, (NB + n_gy - 1) // n_gy)
    cols = BX * BY * NZ // 2
    sims = 2 * NS
    f32 = jnp.float32
    dma = pltpu.SemaphoreType.DMA
    any_spec = pl.BlockSpec(memory_space=pl.ANY)
    vmem = pl.BlockSpec(memory_space=pltpu.VMEM)
    smem = pl.BlockSpec(memory_space=pltpu.SMEM)
    return pl.pallas_call(
        functools.partial(kernel, n_gx, n_gy, cap),
        out_shape=jax.ShapeDtypeStruct((NB, cols), f32),
        in_specs=[any_spec, any_spec, any_spec, smem, smem, vmem, vmem, vmem],
        out_specs=vmem,
        scratch_shapes=[
            pltpu.VMEM((sims, 3, T + 1, X + 8, 128), f32),
            pltpu.VMEM((sims, 3, T + 1, X + 8, 128), f32),
            pltpu.VMEM((T, X, 128), f32),
            pltpu.VMEM((NS, 2, 3, T, X, 128), f32),
            pltpu.VMEM((NS, 3, T, X, 128), f32),
            pltpu.VMEM((T, X, 128), f32),
            pltpu.VMEM((sims, 2, T, 1, 128), f32),
            pltpu.VMEM((sims, 2, T, 1, 128), f32),
            pltpu.VMEM((sims, 2, T, 1, 128), f32),
            pltpu.VMEM((sims, 2, T, 1, 128), f32),
            pltpu.VMEM((2, NB, cols), f32),
            pltpu.VMEM((NB, cols), f32),
            pltpu.VMEM((n_gy, cap, cols), f32),
            pltpu.VMEM((n_gy, cap, cols), f32),
            pltpu.VMEM((n_gy * cap, cols), f32),
            pltpu.VMEM((NB, 3 * NB), jnp.bfloat16),
            pltpu.VMEM((NB, 3 * NB), jnp.bfloat16),
            dma((sims, 2, X // 8)),
            dma((X // 8,)),
            dma((sims,)),
            dma((sims,)),
            dma((sims,)),
            dma((sims,)),
            dma((sims, 2)),
            dma((sims, 2)),
            dma((sims, 2)),
            dma((sims, 2)),
            dma((2,)),
            dma((n_gy,)),
            dma((n_gy,)),
        ],
        compiler_params=pltpu.CompilerParams(
            collective_id=0, has_side_effects=True, vmem_limit_bytes=48 * 1024 * 1024
        ),
    )(
        tiled(forward_state), tiled(adjoint_state), tiled(permittivity),
        waveform, source_cell, block_owner, block_slot, owner_rows,
    )


def solution(mesh):
    in_specs = (
        P("src", None, "gx", "gy"),
        P("src", None, "gx", "gy"),
        P("gx", "gy"),
        P("src", None),
        P("src", None),
        P("gx", "gy"),
        P("gx", "gy"),
        P(("gx", "gy"), None),
    )
    out_specs = P(("gx", "gy"), "src")
    sizes = dict(mesh.shape)
    return jax.shard_map(
        functools.partial(per_device, sizes["gx"], sizes["gy"]),
        mesh=mesh, in_specs=in_specs, out_specs=out_specs, check_vma=False,
    )
```

time: 349 us -> 69.2 us (0.20); the launches traced: 345 us -> 69 us
  local copies, waits for them, and re-layouts: 122 us -> 6.87 us
  starting transfers between devices: 102 us -> 0 us
  other arithmetic: 71.6 us -> 0 us
  Pallas kernels: 0 us -> 62.1 us
  waiting for transfers between devices: 43 us -> 0 us
  blocking collectives: 3.94 us -> 0 us
    ppermute x32 -> x0, starting transfers between devices: 98.3 us -> none  [passed_along(): return lax.ppermute(shard, axis, pairs)]
    slice x81 -> x0, local copies, waits for them, and re-layouts: 62.8 us -> none  [the longest x16 21.3 us: upper_y(): return jnp.concatenate([values[..., z_cells:], ghosts], axis=-1)]
    pallas_call x0 -> x1, Pallas kernels: none -> 62.1 us  [per_device(): pl.pallas_call(functools.partial(kernel, n_gx, n_gy, cap), out_shape=jax....]
    ppermute x32 -> x0, waiting for transfers between devices: 36.9 us -> none  [passed_along(): return lax.ppermute(shard, axis, pairs)]
    sub x11 -> x0, other arithmetic: 26.8 us -> none  [the longest x8 23.2 us: magnetic_update(): magnetic[0]]
    reduce_sum x4 -> x0, other arithmetic: 16 us -> none  [the longest x3 16 us: per_device(): density = density + jnp.sum(intersection, axis=0)]
    another operation x62 -> x0, local copies, waits for them, and re-layouts: 15.6 us -> none  [the longest x16 5.33 us: upper_ghosts(): jnp.stack([electric[0][..., :z_cells], electric[2][..., :z_cells]], axis=1)]
    another operation x32 -> x0, other arithmetic: 13.3 us -> none  [the longest x8 5.79 us: upper_ghosts(): planes = jnp.stack([electric[1][:, :1, :], electric[2][:, :1, :]], axis=1)]
  transfers between devices with their start and end apart: 33 -> 0, of which waited for: 14 -> 0; matrix products, arithmetic and copies ran while one was open for 27% -> 0% of each run, Pallas kernels for 0% -> 0%
where the time goes in v1:
time: 69.2 us; the launch traced here: 69 us
  Pallas kernels  62.1 us (90%)
  local copies, waits for them, and re-layouts  6.87 us (10%)
    pallas_call x1, Pallas kernels, per_device(): pl.pallas_call(functools.partial(kernel, n_gx, n_gy, cap), out_shape=jax....  62.1 us
    unnamed x15, local copies, waits for them, and re-layouts  6.87 us

profile of v1, /device:TPU:0, one launch (start us, length us, event | category | flops | bytes accessed | tf_op | source)
XLA Modules:
  0.0 69.0 jit_solution(18048711377354379120)
XLA Ops:
  0.0 0.0 copy-start
  0.0 1.9 %copy-done = f32[2,6,16,4096]{3,2,1,0:T(8,128)S(1)} copy-done((f32[2,6,16,4096]{3,2,1,0:T(8,128)S(1)}, f32[2,6,16,4096]{3,2,1,0:T(8,128)}, u32[]{:S(2)}) %copy-start) | copy-done | bytes 3145752
  1.9 0.0 copy-start.1
  1.9 0.9 %copy-done.1 = f32[16,4096]{1,0:T(8,128)S(1)} copy-done((f32[16,4096]{1,0:T(8,128)S(1)}, f32[16,4096]{1,0:T(8,128)}, u32[]{:S(2)}) %copy-start.1) | copy-done | bytes 262168
  2.8 0.0 copy-start.2
  2.8 0.7 copy-done.2
  3.5 0.0 copy-start.3
  3.5 0.7 copy-done.3
  4.2 0.0 copy-start.4
  4.2 0.7 copy-done.4
  4.9 0.0 copy-start.5
  4.9 0.7 copy-done.5
  5.6 0.0 copy-start.6
  5.6 0.7 copy-done.6
  6.2 62.1 %shard_map.82 = f32[64,512]{1,0:T(8,128)S(1)} custom-call(f32[2,6,2,32,8,128]{5,4,3,2,1,0:T(8,128)S(1)} %bitcast.9, f32[2,6,2,32,8,128]{5,4,3,2,1,0:T(8,128)} %bitcast.11, f32[2,32,8,128]{3,2,1,0:T(8,128)S(1)} %bitcast.10, f32[2,4]{1,0:T(2,128)S(1)} %copy-done.4, s32[2,3]{1,0:T(2,128)S(1)} %copy-done.5, s32[4,16]{1,0:T(4,128)S(1)} %copy-done.2, ...), custom_call_target="tpu_custom_call" | custom-call | tf_op jit(solution)/shard_map/pallas_call | solution.py:461
  68.3 0.7 copy.10
Async XLA Ops:
  0.0 1.9 %copy-start = (f32[2,6,16,4096]{3,2,1,0:T(8,128)S(1)}, f32[2,6,16,4096]{3,2,1,0:T(8,128)}, u32[]{:S(2)}) copy-start(f32[2,6,16,4096]{3,2,1,0:T(8,128)} %param.8) | copy-start | bytes 9437188
  1.9 0.9 %copy-start.1 = (f32[16,4096]{1,0:T(8,128)S(1)}, f32[16,4096]{1,0:T(8,128)}, u32[]{:S(2)}) copy-start(f32[16,4096]{1,0:T(8,128)} %param.10) | copy-start | bytes 786436
  2.8 0.7 copy-start.2
  3.5 0.7 copy-start.3
  4.2 0.7 copy-start.4
  4.9 0.7 copy-start.5
  5.6 0.7 copy-start.6

commit v2 on v1

--- a/solution.py
+++ b/solution.py
@@ -11,6 +11,7 @@
 STEPS = 4
 BX = 4
 BY = 4
+UNROLL = 8
 COURANT = 0.55
 MESH = pl.DeviceIdType.MESH
 
@@ -25,8 +26,9 @@
 
 def kernel(
     n_gx, n_gy, cap,
-    fwd, adj, perm, wave, cell, owner, slot, rows, out,
+    fwd, adj, perm, wave_hbm, cell_hbm, owner_hbm, slot_hbm, rows_hbm, out,
     E, H, fac, inc, asv, D, SE, SH, GE, GH, B, RB, S2, R2, RF, OH1, OH2,
+    wave, cell, owner, slot, rows, small_sem,
     load_sem, perm_sem,
     exs, exr, hxs, hxr, eys, eyr, hys, hyr, src_sem, rt_s, rt_r,
 ):
@@ -66,6 +68,17 @@
     for sim in range(sims):
         for xt in range(X // 8):
             loads[sim, 1, xt].start()
+    smalls = [
+        pltpu.make_async_copy(a, b, small_sem.at[i])
+        for i, (a, b) in enumerate(
+            (
+                (wave_hbm, wave), (cell_hbm, cell), (owner_hbm, owner),
+                (slot_hbm, slot), (rows_hbm, rows),
+            )
+        )
+    ]
+    for c in smalls:
+        c.start()
     for c in perms:
         c.start()
 
@@ -83,7 +96,7 @@
                 H[sim, c, t + 1, 7:8, :] = zero_row
         return carry
 
-    lax.fori_loop(0, T, zero_ghosts, 0)
+    lax.fori_loop(0, T, zero_ghosts, 0, unroll=4)
 
     barrier = pltpu.get_barrier_semaphore()
     partners = [
@@ -96,6 +109,8 @@
     for device in partners:
         pl.semaphore_signal(barrier, inc=1, device_id=device, device_id_type=MESH)
 
+    for c in smalls:
+        c.wait()
     KB = 3 * NB
     LBY = owner.shape[1]
     dest = jnp.where(owner[...] >= 0, owner[...] * cap + slot[...], -1)
@@ -210,7 +225,7 @@
                 E[sim, 2, t, X : X + 1, :] = GE[sim, 1, t]
                 return carry
 
-            lax.fori_loop(0, T, unpack, 0, unroll=8)
+            lax.fori_loop(0, T, unpack, 0, unroll=True)
 
         @pl.when(gy < n_gy - 1)
         def _():
@@ -229,7 +244,7 @@
                 H[sim, 2, t + 1, 7:8, :] = GH[sim, 1, t]
                 return carry
 
-            lax.fori_loop(0, T, unpack, 0, unroll=8)
+            lax.fori_loop(0, T, unpack, 0, unroll=True)
 
         @pl.when(gy > 0)
         def _():
@@ -245,7 +260,7 @@
     cells_yz = T * 128
     linear = row * cells_yz + lane
 
-    def h_phase(sim):
+    def h_phase(sim, step):
         def tile(t):
             ex = E[sim, 0, t, 0:X, :]
             ey = E[sim, 1, t, 0:X, :]
@@ -261,9 +276,13 @@
             hx = H[sim, 0, t + 1, 8 : 8 + X, :]
             hy = H[sim, 1, t + 1, 8 : 8 + X, :]
             hz = H[sim, 2, t + 1, 8 : 8 + X, :]
-            hx = hx - COURANT * ((ezy - ez) - (eyz - ey))
-            hy = hy - COURANT * ((exz - ex) - (ezx - ez))
-            hz = hz - COURANT * ((eyx - ey) - (exy - ex))
+            if step == 0:
+                hx = hx * (1.0 / COURANT)
+                hy = hy * (1.0 / COURANT)
+                hz = hz * (1.0 / COURANT)
+            hx = hx - ((ezy - ez) - (eyz - ey))
+            hy = hy - ((exz - ex) - (ezx - ez))
+            hz = hz - ((eyx - ey) - (exy - ex))
             H[sim, 0, t + 1, 8 : 8 + X, :] = hx
             H[sim, 1, t + 1, 8 : 8 + X, :] = hy
             H[sim, 2, t + 1, 8 : 8 + X, :] = hz
@@ -271,11 +290,11 @@
             SH[sim, 1, t] = hz[X - 1 : X, :]
 
         def body(i, carry):
-            tile(2 * i)
-            tile(2 * i + 1)
+            for k in range(UNROLL):
+                tile(UNROLL * i + k)
             return carry
 
-        lax.fori_loop(0, T // 2, body, 0)
+        lax.fori_loop(0, T // UNROLL, body, 0)
 
     def e_phase(sim, step):
         s = sim % NS
@@ -342,15 +361,15 @@
                         e0 * inc[s, k, 0, t] + e1 * inc[s, k, 1, t] + e2 * inc[s, k, 2, t]
                     )
                     if step == STEPS - 1 and s == NS - 1:
-                        total = total * (f * (-1.0 / COURANT))
+                        total = total * (f * (-1.0 / (COURANT * COURANT)))
                     D[t] = total
 
         def body(i, carry):
-            tile(2 * i)
-            tile(2 * i + 1)
+            for k in range(UNROLL):
+                tile(UNROLL * i + k)
             return carry
 
-        lax.fori_loop(0, T // 2, body, 0)
+        lax.fori_loop(0, T // UNROLL, body, 0)
 
     pl.semaphore_wait(barrier, len(partners))
     for sim in range(sims):
@@ -362,17 +381,17 @@
             SE[sim, 1, t] = E[sim, 2, t, 0:1, :]
             return carry
 
-        lax.fori_loop(0, T, pack, 0, unroll=8)
+        lax.fori_loop(0, T, pack, 0, unroll=True)
         e_send(sim)
 
     for c in perms:
         c.wait()
 
     def make_factor(t, carry):
-        fac[t] = COURANT / fac[t]
+        fac[t] = (COURANT * COURANT) / fac[t]
         return carry
 
-    lax.fori_loop(0, T, make_factor, 0)
+    lax.fori_loop(0, T, make_factor, 0, unroll=8)
 
     for step in range(STEPS):
         for sim in range(sims):
@@ -382,7 +401,7 @@
             e_arrive(sim)
             if step > 0:
                 h_sent(sim)
-            h_phase(sim)
+            h_phase(sim, step)
             h_send(sim)
         for sim in range(sims):
             h_arrive(sim)
@@ -457,11 +476,10 @@
     dma = pltpu.SemaphoreType.DMA
     any_spec = pl.BlockSpec(memory_space=pl.ANY)
     vmem = pl.BlockSpec(memory_space=pltpu.VMEM)
-    smem = pl.BlockSpec(memory_space=pltpu.SMEM)
     return pl.pallas_call(
         functools.partial(kernel, n_gx, n_gy, cap),
         out_shape=jax.ShapeDtypeStruct((NB, cols), f32),
-        in_specs=[any_spec, any_spec, any_spec, smem, smem, vmem, vmem, vmem],
+        in_specs=[any_spec] * 8,
         out_specs=vmem,
         scratch_shapes=[
             pltpu.VMEM((sims, 3, T + 1, X + 8, 128), f32),
@@ -481,6 +499,12 @@
             pltpu.VMEM((n_gy * cap, cols), f32),
             pltpu.VMEM((NB, 3 * NB), jnp.bfloat16),
             pltpu.VMEM((NB, 3 * NB), jnp.bfloat16),
+            pltpu.SMEM(waveform.shape, f32),
+            pltpu.SMEM(source_cell.shape, jnp.int32),
+            pltpu.VMEM(block_owner.shape, jnp.int32),
+            pltpu.VMEM(block_slot.shape, jnp.int32),
+            pltpu.VMEM(owner_rows.shape, jnp.int32),
+            dma((5,)),
             dma((sims, 2, X // 8)),
             dma((X // 8,)),
             dma((sims,)),
@@ -496,7 +520,7 @@
             dma((n_gy,)),
         ],
         compiler_params=pltpu.CompilerParams(
-            collective_id=0, has_side_effects=True, vmem_limit_bytes=48 * 1024 * 1024
+            collective_id=0, has_side_effects=True, vmem_limit_bytes=62 * 1024 * 1024
         ),
     )(
         tiled(forward_state), tiled(adjoint_state), tiled(permittivity),

time: 69.2 us -> 44.7 us (0.65)
  Pallas kernels: 62.1 us -> 42.9 us
  local copies, waits for them, and re-layouts: 6.87 us -> 1.57 us
    pallas_call x1, Pallas kernels: 62.1 us -> 42.9 us  [per_device(): pl.pallas_call(functools.partial(kernel, n_gx, n_gy, cap), out_shape=jax....]
    unnamed x15 -> x1, local copies, waits for them, and re-layouts: 6.87 us -> 1.57 us
where the time goes in v2:
time: 44.7 us; the launch traced here: 44.5 us
  Pallas kernels  42.9 us (96%)
  local copies, waits for them, and re-layouts  1.57 us (4%)
    pallas_call x1, Pallas kernels, per_device(): pl.pallas_call(functools.partial(kernel, n_gx, n_gy, cap), out_shape=jax....  42.9 us
    unnamed x1, local copies, waits for them, and re-layouts  1.57 us

profile of v2, /device:TPU:0, one launch (start us, length us, event | category | flops | bytes accessed | tf_op | source)
XLA Modules:
  0.0 44.5 jit_solution(9598152483010314290)
XLA Ops:
  0.0 42.9 %shard_map.82 = f32[64,512]{1,0:T(8,128)} custom-call(f32[2,6,2,32,8,128]{5,4,3,2,1,0:T(8,128)} %bitcast.9, f32[2,6,2,32,8,128]{5,4,3,2,1,0:T(8,128)} %bitcast.10, f32[2,32,8,128]{3,2,1,0:T(8,128)} %bitcast.11, f32[2,4]{1,0:T(2,128)} %wave_hbm.1, s32[2,3]{1,0:T(2,128)} %cell_hbm.1, s32[4,16]{1,0:T(4,128)} %owner_hbm.1, s32[4,16]{1,0:T(4,128)} %slot_hbm.1, ...), custom_call_target="tpu_custom_call" | custom-call | tf_op jit(solution)/shard_map/pallas_call | solution.py:479
  42.9 1.6 %copy.10 = f32[64,512]{1,0:T(8,128)} copy(f32[64,512]{1,0:T(8,128)} %shard_map.82) | data formatting | bytes 262144

commit v3 on v2

--- a/solution.py
+++ b/solution.py
@@ -27,7 +27,7 @@
 def kernel(
     n_gx, n_gy, cap,
     fwd, adj, perm, wave_hbm, cell_hbm, owner_hbm, slot_hbm, rows_hbm, out,
-    E, H, fac, inc, asv, D, SE, SH, GE, GH, B, RB, S2, R2, RF, OH1, OH2,
+    ST, PS, YE, YH, E, H, fac, inc, asv, D, SE, SH, GE, GH, B, RB, S2, R2, RF, OH1, OH2,
     wave, cell, owner, slot, rows, small_sem,
     load_sem, perm_sem,
     exs, exr, hxs, hxr, eys, eyr, hys, hyr, src_sem, rt_s, rt_r,
@@ -48,17 +48,17 @@
         for xt in range(X // 8):
             loads[sim, 0, xt] = pltpu.make_async_copy(
                 state.at[s, pl.ds(0, 3), xt],
-                E.at[sim, :, pl.ds(0, T), pl.ds(8 * xt, 8), :],
+                ST.at[sim, pl.ds(0, 3), :, pl.ds(8 * xt, 8), :],
                 load_sem.at[sim, 0, xt],
             )
             loads[sim, 1, xt] = pltpu.make_async_copy(
                 state.at[s, pl.ds(3, 3), xt],
-                H.at[sim, :, pl.ds(1, T), pl.ds(8 + 8 * xt, 8), :],
+                ST.at[sim, pl.ds(3, 3), :, pl.ds(8 * xt, 8), :],
                 load_sem.at[sim, 1, xt],
             )
     perms = [
         pltpu.make_async_copy(
-            perm.at[xt], fac.at[:, pl.ds(8 * xt, 8), :], perm_sem.at[xt]
+            perm.at[xt], PS.at[:, pl.ds(8 * xt, 8), :], perm_sem.at[xt]
         )
         for xt in range(X // 8)
     ]
@@ -82,21 +82,24 @@
     for c in perms:
         c.start()
 
+    R = X + 8
+    EF = E.reshape(sims * 3 * (T + 1) * R, 128)
+    HF = H.reshape(sims * 3 * (T + 1) * R, 128)
+
+    def e_row(sim, c, r):
+        return pl.ds((sim * 3 + c) * (T + 1) * R + r, T, stride=R), slice(None)
+
+    def h_row(sim, c, r):
+        return e_row(sim, c, R + r)
+
     zero_tile = jnp.zeros((X, 128), jnp.float32)
-    zero_row = jnp.zeros((1, 128), jnp.float32)
-    for sim in range(sims):
-        for c in (0, 2):
-            E[sim, c, T, 0:X, :] = zero_tile
-            H[sim, c, 0, 8 : 8 + X, :] = zero_tile
-
-    def zero_ghosts(t, carry):
-        for sim in range(sims):
-            for c in (1, 2):
-                E[sim, c, t, X : X + 1, :] = zero_row
-                H[sim, c, t + 1, 7:8, :] = zero_row
-        return carry
-
-    lax.fori_loop(0, T, zero_ghosts, 0, unroll=4)
+    zero_rows = jnp.zeros((T, 128), jnp.float32)
+    for sim in range(sims):
+        for i in range(2):
+            YE[sim, i] = zero_tile
+            YH[sim, i] = zero_tile
+            EF[e_row(sim, 1 + i, X)] = zero_rows
+            HF[h_row(sim, 1 + i, 7)] = zero_rows
 
     barrier = pltpu.get_barrier_semaphore()
     partners = [
@@ -133,6 +136,15 @@
     line = jnp.dot(row8, pick, preferred_element_type=jnp.float32)[0:1, :]
     OH2[...] = jnp.where(line == r_f, 1.0, 0.0).astype(jnp.bfloat16)
 
+    lane = lax.broadcasted_iota(jnp.int32, (X, 128), 1)
+    row = lax.broadcasted_iota(jnp.int32, (X, 128), 0)
+    z = lane % NZ
+    z_first = z == 0
+    z_last = z == NZ - 1
+    low = lane < NZ
+    cells_yz = T * 128
+    linear = row * cells_yz + jnp.where(low, z, z + T * NZ)
+
     def e_copies(sim):
         x = pltpu.make_async_remote_copy(
             SE.at[sim], GE.at[sim], exs.at[sim], exr.at[sim],
@@ -141,7 +153,7 @@
         ys = [
             pltpu.make_async_remote_copy(
                 E.at[sim, c, 0, pl.ds(0, X), :],
-                E.at[sim, c, T, pl.ds(0, X), :],
+                YE.at[sim, i],
                 eys.at[sim, i], eyr.at[sim, i],
                 device_id={"gy": gy - 1}, device_id_type=MESH,
             )
@@ -157,7 +169,7 @@
         ys = [
             pltpu.make_async_remote_copy(
                 H.at[sim, c, T, pl.ds(8, X), :],
-                H.at[sim, c, 0, pl.ds(8, X), :],
+                YH.at[sim, i],
                 hys.at[sim, i], hyr.at[sim, i],
                 device_id={"gy": gy + 1}, device_id_type=MESH,
             )
@@ -219,82 +231,69 @@
         @pl.when(gx < n_gx - 1)
         def _():
             x.wait_recv()
-
-            def unpack(t, carry):
-                E[sim, 1, t, X : X + 1, :] = GE[sim, 0, t]
-                E[sim, 2, t, X : X + 1, :] = GE[sim, 1, t]
-                return carry
-
-            lax.fori_loop(0, T, unpack, 0, unroll=True)
+            for i in range(2):
+                EF[e_row(sim, 1 + i, X)] = GE[sim, i]
 
         @pl.when(gy < n_gy - 1)
         def _():
             for y in ys:
                 y.wait_recv()
 
+        for i, c in enumerate((0, 2)):
+            edge = jnp.where(low, YE[sim, i], E[sim, c, 0, 0:X, :])
+            E[sim, c, T, 0:X, :] = pltpu.roll(edge, NZ, 1)
+
     def h_arrive(sim):
         x, ys = h_copies(sim)
 
         @pl.when(gx > 0)
         def _():
             x.wait_recv()
-
-            def unpack(t, carry):
-                H[sim, 1, t + 1, 7:8, :] = GH[sim, 0, t]
-                H[sim, 2, t + 1, 7:8, :] = GH[sim, 1, t]
-                return carry
-
-            lax.fori_loop(0, T, unpack, 0, unroll=True)
+            for i in range(2):
+                HF[h_row(sim, 1 + i, 7)] = GH[sim, i]
 
         @pl.when(gy > 0)
         def _():
             for y in ys:
                 y.wait_recv()
 
-    lane = lax.broadcasted_iota(jnp.int32, (X, 128), 1)
-    row = lax.broadcasted_iota(jnp.int32, (X, 128), 0)
-    z = lane % NZ
-    z_first = z == 0
-    z_last = z == NZ - 1
-    low = lane < NZ
-    cells_yz = T * 128
-    linear = row * cells_yz + lane
-
-    def h_phase(sim, step):
-        def tile(t):
-            ex = E[sim, 0, t, 0:X, :]
+        for i, c in enumerate((0, 2)):
+            edge = jnp.where(low, H[sim, c, T, 8 : 8 + X, :], YH[sim, i])
+            H[sim, c, 0, 8 : 8 + X, :] = pltpu.roll(edge, NZ, 1)
+
+    def h_phase(sim):
+        def tile(t, held):
+            ex, ez = held
             ey = E[sim, 1, t, 0:X, :]
-            ez = E[sim, 2, t, 0:X, :]
             exn = E[sim, 0, t + 1, 0:X, :]
             ezn = E[sim, 2, t + 1, 0:X, :]
             eyx = E[sim, 1, t, 1 : X + 1, :]
             ezx = E[sim, 2, t, 1 : X + 1, :]
-            exy = pltpu.roll(jnp.where(low, exn, ex), NZ, 1)
-            ezy = pltpu.roll(jnp.where(low, ezn, ez), NZ, 1)
             exz = jnp.where(z_last, 0.0, pltpu.roll(ex, 127, 1))
             eyz = jnp.where(z_last, 0.0, pltpu.roll(ey, 127, 1))
             hx = H[sim, 0, t + 1, 8 : 8 + X, :]
             hy = H[sim, 1, t + 1, 8 : 8 + X, :]
             hz = H[sim, 2, t + 1, 8 : 8 + X, :]
-            if step == 0:
-                hx = hx * (1.0 / COURANT)
-                hy = hy * (1.0 / COURANT)
-                hz = hz * (1.0 / COURANT)
-            hx = hx - ((ezy - ez) - (eyz - ey))
+            hx = hx - ((ezn - ez) - (eyz - ey))
             hy = hy - ((exz - ex) - (ezx - ez))
-            hz = hz - ((eyx - ey) - (exy - ex))
+            hz = hz - ((eyx - ey) - (exn - ex))
             H[sim, 0, t + 1, 8 : 8 + X, :] = hx
             H[sim, 1, t + 1, 8 : 8 + X, :] = hy
             H[sim, 2, t + 1, 8 : 8 + X, :] = hz
-            SH[sim, 0, t] = hy[X - 1 : X, :]
-            SH[sim, 1, t] = hz[X - 1 : X, :]
+            return exn, ezn
 
         def body(i, carry):
+            held = (
+                E[sim, 0, UNROLL * i, 0:X, :],
+                E[sim, 2, UNROLL * i, 0:X, :],
+            )
             for k in range(UNROLL):
-                tile(UNROLL * i + k)
+                held = tile(UNROLL * i + k, held)
             return carry
 
         lax.fori_loop(0, T // UNROLL, body, 0)
+        for i in range(2):
+            SH[sim, i] = HF[h_row(sim, 1 + i, 7 + X)]
 
     def e_phase(sim, step):
         s = sim % NS
@@ -306,24 +305,21 @@
             target = jnp.where(inside, lx * cells_yz + lyz, -1)
             pulse = wave[s, step]
 
-        def tile(t):
+        def tile(t, held):
+            hxp, hzp = held
             hx = H[sim, 0, t + 1, 8 : 8 + X, :]
             hy = H[sim, 1, t + 1, 8 : 8 + X, :]
             hz = H[sim, 2, t + 1, 8 : 8 + X, :]
-            hxp = H[sim, 0, t, 8 : 8 + X, :]
-            hzp = H[sim, 2, t, 8 : 8 + X, :]
             hyx = H[sim, 1, t + 1, 7 : 7 + X, :]
             hzx = H[sim, 2, t + 1, 7 : 7 + X, :]
-            hxy = pltpu.roll(jnp.where(low, hx, hxp), NZ, 1)
-            hzy = pltpu.roll(jnp.where(low, hz, hzp), NZ, 1)
             hxz = jnp.where(z_first, 0.0, pltpu.roll(hx, 1, 1))
             hyz = jnp.where(z_first, 0.0, pltpu.roll(hy, 1, 1))
             f = fac[t]
-            d0 = f * ((hz - hzy) - (hy - hyz))
+            d0 = f * ((hz - hzp) - (hy - hyz))
             d1 = f * ((hx - hxz) - (hz - hzx))
-            d2 = f * ((hy - hyx) - (hx - hxy))
+            d2 = f * ((hy - hyx) - (hx - hxp))
             if forward:
-                hit = linear == target - t * 128
+                hit = linear == target - t * NZ
                 d2 = d2 + jnp.where(hit, pulse, 0.0)
             if not (forward and step == STEPS - 1):
                 e0 = E[sim, 0, t, 0:X, :] + d0
@@ -333,8 +329,6 @@
                 E[sim, 0, t, 0:X, :] = e0
                 E[sim, 1, t, 0:X, :] = e1
                 E[sim, 2, t, 0:X, :] = e2
-                SE[sim, 0, t] = e1[0:1, :]
-                SE[sim, 1, t] = e2[0:1, :]
             if forward:
                 if step < 2:
                     inc[s, step, 0, t] = d0
@@ -363,45 +357,75 @@
                     if step == STEPS - 1 and s == NS - 1:
                         total = total * (f * (-1.0 / (COURANT * COURANT)))
                     D[t] = total
+            return hx, hz
 
         def body(i, carry):
+            held = (
+                H[sim, 0, UNROLL * i, 8 : 8 + X, :],
+                H[sim, 2, UNROLL * i, 8 : 8 + X, :],
+            )
             for k in range(UNROLL):
-                tile(UNROLL * i + k)
+                held = tile(UNROLL * i + k, held)
             return carry
 
         lax.fori_loop(0, T // UNROLL, body, 0)
+        if step < STEPS - 1:
+            e_pack(sim)
+
+    def e_pack(sim):
+        for i in range(2):
+            SE[sim, i] = EF[e_row(sim, 1 + i, 0)]
+
+    def halves(lo, hi):
+        even = jnp.where(low, lo, pltpu.roll(hi, NZ, 1))
+        odd = jnp.where(low, pltpu.roll(lo, NZ, 1), hi)
+        return even, odd
 
     pl.semaphore_wait(barrier, len(partners))
     for sim in range(sims):
         for xt in range(X // 8):
             loads[sim, 0, xt].wait()
 
-        def pack(t, carry):
-            SE[sim, 0, t] = E[sim, 1, t, 0:1, :]
-            SE[sim, 1, t] = E[sim, 2, t, 0:1, :]
+        def e_layout(a, carry):
+            for c in range(3):
+                even, odd = halves(ST[sim, c, a], ST[sim, c, a + T // 2])
+                E[sim, c, 2 * a, 0:X, :] = even
+                E[sim, c, 2 * a + 1, 0:X, :] = odd
             return carry
 
-        lax.fori_loop(0, T, pack, 0, unroll=True)
+        lax.fori_loop(0, T // 2, e_layout, 0, unroll=4)
+        e_pack(sim)
         e_send(sim)
 
     for c in perms:
         c.wait()
 
-    def make_factor(t, carry):
-        fac[t] = (COURANT * COURANT) / fac[t]
+    def make_factor(a, carry):
+        even, odd = halves(PS[a], PS[a + T // 2])
+        fac[2 * a] = (COURANT * COURANT) / even
+        fac[2 * a + 1] = (COURANT * COURANT) / odd
         return carry
 
-    lax.fori_loop(0, T, make_factor, 0, unroll=8)
+    lax.fori_loop(0, T // 2, make_factor, 0, unroll=4)
+    for sim in range(sims):
+        for xt in range(X // 8):
+            loads[sim, 1, xt].wait()
+
+        def h_layout(a, carry):
+            for c in range(3):
+                even, odd = halves(ST[sim, 3 + c, a], ST[sim, 3 + c, a + T // 2])
+                H[sim, c, 2 * a + 1, 8 : 8 + X, :] = even * (1.0 / COURANT)
+                H[sim, c, 2 * a + 2, 8 : 8 + X, :] = odd * (1.0 / COURANT)
+            return carry
+
+        lax.fori_loop(0, T // 2, h_layout, 0, unroll=4)
 
     for step in range(STEPS):
         for sim in range(sims):
-            if step == 0:
-                for xt in range(X // 8):
-                    loads[sim, 1, xt].wait()
             e_arrive(sim)
             if step > 0:
                 h_sent(sim)
-            h_phase(sim, step)
+            h_phase(sim)
             h_send(sim)
         for sim in range(sims):
             h_arrive(sim)
@@ -412,6 +436,11 @@
     for sim in range(sims):
         h_sent(sim)
 
+    def d_layout(a, carry):
+        PS[a], PS[a + T // 2] = halves(D[2 * a], D[2 * a + 1])
+        return carry
+
+    lax.fori_loop(0, T // 2, d_layout, 0, unroll=4)
     half = BX // 2
     for h in range(2):
         for p in range(X // BX):
@@ -419,7 +448,7 @@
                 for yh in range(BY // 2):
                     j = xi * (BY // 2) + yh
                     start = yh * X + BX * p + half * h + xi
-                    B[h, p * LBY : (p + 1) * LBY, j * 128 : (j + 1) * 128] = D.reshape(
+                    B[h, p * LBY : (p + 1) * LBY, j * 128 : (j + 1) * 128] = PS.reshape(
                         T * X, 128
                     )[pl.ds(start, LBY, stride=2 * X), :]
     peer = pltpu.make_async_remote_copy(
@@ -482,16 +511,20 @@
         in_specs=[any_spec] * 8,
         out_specs=vmem,
         scratch_shapes=[
+            pltpu.VMEM((sims, 6, T, X, 128), f32),
+            pltpu.VMEM((T, X, 128), f32),
+            pltpu.VMEM((sims, 2, X, 128), f32),
+            pltpu.VMEM((sims, 2, X, 128), f32),
             pltpu.VMEM((sims, 3, T + 1, X + 8, 128), f32),
             pltpu.VMEM((sims, 3, T + 1, X + 8, 128), f32),
             pltpu.VMEM((T, X, 128), f32),
             pltpu.VMEM((NS, 2, 3, T, X, 128), f32),
             pltpu.VMEM((NS, 3, T, X, 128), f32),
             pltpu.VMEM((T, X, 128), f32),
-            pltpu.VMEM((sims, 2, T, 1, 128), f32),
-            pltpu.VMEM((sims, 2, T, 1, 128), f32),
-            pltpu.VMEM((sims, 2, T, 1, 128), f32),
-            pltpu.VMEM((sims, 2, T, 1, 128), f32),
+            pltpu.VMEM((sims, 2, T, 128), f32),
+            pltpu.VMEM((sims, 2, T, 128), f32),
+            pltpu.VMEM((sims, 2, T, 128), f32),
+            pltpu.VMEM((sims, 2, T, 128), f32),
             pltpu.VMEM((2, NB, cols), f32),
             pltpu.VMEM((NB, cols), f32),
             pltpu.VMEM((n_gy, cap, cols), f32),

time: 44.7 us -> 45.9 us (1.027)
  Pallas kernels: 42.9 us -> 44.2 us
    pallas_call x1, Pallas kernels: 42.9 us -> 44.2 us  [per_device(): pl.pallas_call(functools.partial(kernel, n_gx, n_gy, cap), out_shape=jax....]
where the time goes in v3:
time: 45.9 us; the launch traced here: 45.7 us
  Pallas kernels  44.2 us (96%)
  local copies, waits for them, and re-layouts  1.57 us (3%)
    pallas_call x1, Pallas kernels, per_device(): pl.pallas_call(functools.partial(kernel, n_gx, n_gy, cap), out_shape=jax....  44.2 us
    unnamed x1, local copies, waits for them, and re-layouts  1.57 us

profile of v3, /device:TPU:0, one launch (start us, length us, event | category | flops | bytes accessed | tf_op | source)
XLA Modules:
  0.0 45.7 jit_solution(3552191165519782301)
XLA Ops:
  0.0 44.2 %shard_map.82 = f32[64,512]{1,0:T(8,128)} custom-call(f32[2,6,2,32,8,128]{5,4,3,2,1,0:T(8,128)} %bitcast.9, f32[2,6,2,32,8,128]{5,4,3,2,1,0:T(8,128)} %bitcast.10, f32[2,32,8,128]{3,2,1,0:T(8,128)} %bitcast.11, f32[2,4]{1,0:T(2,128)} %wave_hbm.1, s32[2,3]{1,0:T(2,128)} %cell_hbm.1, s32[4,16]{1,0:T(4,128)} %owner_hbm.1, s32[4,16]{1,0:T(4,128)} %slot_hbm.1, ...), custom_call_target="tpu_custom_call" | custom-call | tf_op jit(solution)/shard_map/pallas_call | solution.py:508
  44.2 1.6 %copy.10 = f32[64,512]{1,0:T(8,128)} copy(f32[64,512]{1,0:T(8,128)} %shard_map.82) | data formatting | bytes 262144

commit v4 on v3

--- a/solution.py
+++ b/solution.py
@@ -11,7 +11,7 @@
 STEPS = 4
 BX = 4
 BY = 4
-UNROLL = 8
+CHUNKS = 4
 COURANT = 0.55
 MESH = pl.DeviceIdType.MESH
 
@@ -86,11 +86,14 @@
     EF = E.reshape(sims * 3 * (T + 1) * R, 128)
     HF = H.reshape(sims * 3 * (T + 1) * R, 128)
 
-    def e_row(sim, c, r):
-        return pl.ds((sim * 3 + c) * (T + 1) * R + r, T, stride=R), slice(None)
-
-    def h_row(sim, c, r):
-        return e_row(sim, c, R + r)
+    TC = T // CHUNKS
+
+    def e_row(sim, c, r, t=0, n=TC):
+        start = ((sim * 3 + c) * (T + 1) + t) * R + r
+        return pl.ds(start, n, stride=R), slice(None)
+
+    def h_row(sim, c, r, t=0, n=TC):
+        return e_row(sim, c, r, t + 1, n)
 
     zero_tile = jnp.zeros((X, 128), jnp.float32)
     zero_rows = jnp.zeros((T, 128), jnp.float32)
@@ -98,8 +101,8 @@
         for i in range(2):
             YE[sim, i] = zero_tile
             YH[sim, i] = zero_tile
-            EF[e_row(sim, 1 + i, X)] = zero_rows
-            HF[h_row(sim, 1 + i, 7)] = zero_rows
+            EF[e_row(sim, 1 + i, X, 0, T)] = zero_rows
+            HF[h_row(sim, 1 + i, 7, 0, T)] = zero_rows
 
     barrier = pltpu.get_barrier_semaphore()
     partners = [
@@ -145,12 +148,20 @@
     cells_yz = T * 128
     linear = row * cells_yz + jnp.where(low, z, z + T * NZ)
 
-    def e_copies(sim):
-        x = pltpu.make_async_remote_copy(
-            SE.at[sim], GE.at[sim], exs.at[sim], exr.at[sim],
+    def e_x(sim, q):
+        return pltpu.make_async_remote_copy(
+            SE.at[sim, q], GE.at[sim, q], exs.at[sim, q], exr.at[sim, q],
             device_id={"gx": gx - 1}, device_id_type=MESH,
         )
-        ys = [
+
+    def h_x(sim, q):
+        return pltpu.make_async_remote_copy(
+            SH.at[sim, q], GH.at[sim, q], hxs.at[sim, q], hxr.at[sim, q],
+            device_id={"gx": gx + 1}, device_id_type=MESH,
+        )
+
+    def e_ys(sim):
+        return [
             pltpu.make_async_remote_copy(
                 E.at[sim, c, 0, pl.ds(0, X), :],
                 YE.at[sim, i],
@@ -159,14 +170,9 @@
             )
             for i, c in enumerate((0, 2))
         ]
-        return x, ys
-
-    def h_copies(sim):
-        x = pltpu.make_async_remote_copy(
-            SH.at[sim], GH.at[sim], hxs.at[sim], hxr.at[sim],
-            device_id={"gx": gx + 1}, device_id_type=MESH,
-        )
-        ys = [
+
+    def h_ys(sim):
+        return [
             pltpu.make_async_remote_copy(
                 H.at[sim, c, T, pl.ds(8, X), :],
                 YH.at[sim, i],
@@ -175,86 +181,88 @@
             )
             for i, c in enumerate((0, 2))
         ]
-        return x, ys
-
-    def e_send(sim):
-        x, ys = e_copies(sim)
-
-        @pl.when(gx > 0)
-        def _():
-            x.start()
-
-        @pl.when(gy > 0)
-        def _():
-            for y in ys:
+
+    down_x, up_x = gx > 0, gx < n_gx - 1
+    down_y, up_y = gy > 0, gy < n_gy - 1
+
+    def e_send_x(sim, q):
+        for i in range(2):
+            SE[sim, q, i] = EF[e_row(sim, 1 + i, 0, q * TC)]
+
+        @pl.when(down_x)
+        def _():
+            e_x(sim, q).start()
+
+    def h_send_x(sim, q):
+        for i in range(2):
+            SH[sim, q, i] = HF[h_row(sim, 1 + i, 7 + X, q * TC)]
+
+        @pl.when(up_x)
+        def _():
+            h_x(sim, q).start()
+
+    def e_send_y(sim):
+        @pl.when(down_y)
+        def _():
+            for y in e_ys(sim):
                 y.start()
 
+    def h_send_y(sim):
+        @pl.when(up_y)
+        def _():
+            for y in h_ys(sim):
+                y.start()
+
     def e_sent(sim):
-        x, ys = e_copies(sim)
-
-        @pl.when(gx > 0)
-        def _():
-            x.wait_send()
-
-        @pl.when(gy > 0)
-        def _():
-            for y in ys:
+        @pl.when(down_x)
+        def _():
+            for q in range(CHUNKS):
+                e_x(sim, q).wait_send()
+
+        @pl.when(down_y)
+        def _():
+            for y in e_ys(sim):
                 y.wait_send()
 
-    def h_send(sim):
-        x, ys = h_copies(sim)
-
-        @pl.when(gx < n_gx - 1)
-        def _():
-            x.start()
-
-        @pl.when(gy < n_gy - 1)
-        def _():
-            for y in ys:
-                y.start()
-
     def h_sent(sim):
-        x, ys = h_copies(sim)
-
-        @pl.when(gx < n_gx - 1)
-        def _():
-            x.wait_send()
-
-        @pl.when(gy < n_gy - 1)
-        def _():
-            for y in ys:
+        @pl.when(up_x)
+        def _():
+            for q in range(CHUNKS):
+                h_x(sim, q).wait_send()
+
+        @pl.when(up_y)
+        def _():
+            for y in h_ys(sim):
                 y.wait_send()
 
-    def e_arrive(sim):
-        x, ys = e_copies(sim)
-
-        @pl.when(gx < n_gx - 1)
-        def _():
-            x.wait_recv()
+    def e_arrive_x(sim, q):
+        @pl.when(up_x)
+        def _():
+            e_x(sim, q).wait_recv()
             for i in range(2):
-                EF[e_row(sim, 1 + i, X)] = GE[sim, i]
-
-        @pl.when(gy < n_gy - 1)
-        def _():
-            for y in ys:
+                EF[e_row(sim, 1 + i, X, q * TC)] = GE[sim, q, i]
+
+    def h_arrive_x(sim, q):
+        @pl.when(down_x)
+        def _():
+            h_x(sim, q).wait_recv()
+            for i in range(2):
+                HF[h_row(sim, 1 + i, 7, q * TC)] = GH[sim, q, i]
+
+    def e_arrive_y(sim):
+        @pl.when(up_y)
+        def _():
+            for y in e_ys(sim):
                 y.wait_recv()
 
         for i, c in enumerate((0, 2)):
             edge = jnp.where(low, YE[sim, i], E[sim, c, 0, 0:X, :])
             E[sim, c, T, 0:X, :] = pltpu.roll(edge, NZ, 1)
 
-    def h_arrive(sim):
-        x, ys = h_copies(sim)
-
-        @pl.when(gx > 0)
-        def _():
-            x.wait_recv()
-            for i in range(2):
-                HF[h_row(sim, 1 + i, 7)] = GH[sim, i]
-
-        @pl.when(gy > 0)
-        def _():
-            for y in ys:
+    def h_arrive_y(sim):
+        @pl.when(down_y)
+        def _():
+            for y in h_ys(sim):
                 y.wait_recv()
 
         for i, c in enumerate((0, 2)):
@@ -283,17 +291,21 @@
             return exn, ezn
 
         def body(i, carry):
-            held = (
-                E[sim, 0, UNROLL * i, 0:X, :],
-                E[sim, 2, UNROLL * i, 0:X, :],
-            )
-            for k in range(UNROLL):
-                held = tile(UNROLL * i + k, held)
+            q = lax.rem(i + CHUNKS - 1, CHUNKS)
+            e_arrive_x(sim, q)
+            t = q * TC
+            held = E[sim, 0, t, 0:X, :], E[sim, 2, t, 0:X, :]
+            for k in range(TC):
+                held = tile(t + k, held)
+            h_send_x(sim, q)
+
+            @pl.when(i == 0)
+            def _():
+                h_send_y(sim)
+
             return carry
 
-        lax.fori_loop(0, T // UNROLL, body, 0)
-        for i in range(2):
-            SH[sim, i] = HF[h_row(sim, 1 + i, 7 + X)]
+        lax.fori_loop(0, CHUNKS, body, 0)
 
     def e_phase(sim, step):
         s = sim % NS
@@ -360,21 +372,22 @@
             return hx, hz
 
         def body(i, carry):
-            held = (
-                H[sim, 0, UNROLL * i, 8 : 8 + X, :],
-                H[sim, 2, UNROLL * i, 8 : 8 + X, :],
-            )
-            for k in range(UNROLL):
-                held = tile(UNROLL * i + k, held)
+            q = lax.rem(CHUNKS - i, CHUNKS)
+            h_arrive_x(sim, q)
+            t = q * TC
+            held = H[sim, 0, t, 8 : 8 + X, :], H[sim, 2, t, 8 : 8 + X, :]
+            for k in range(TC):
+                held = tile(t + k, held)
+            if step < STEPS - 1:
+                e_send_x(sim, q)
+
+                @pl.when(i == 0)
+                def _():
+                    e_send_y(sim)
+
             return carry
 
-        lax.fori_loop(0, T // UNROLL, body, 0)
-        if step < STEPS - 1:
-            e_pack(sim)
-
-    def e_pack(sim):
-        for i in range(2):
-            SE[sim, i] = EF[e_row(sim, 1 + i, 0)]
+        lax.fori_loop(0, CHUNKS, body, 0)
 
     def halves(lo, hi):
         even = jnp.where(low, lo, pltpu.roll(hi, NZ, 1))
@@ -394,8 +407,9 @@
             return carry
 
         lax.fori_loop(0, T // 2, e_layout, 0, unroll=4)
-        e_pack(sim)
-        e_send(sim)
+        e_send_y(sim)
+        for i in range(CHUNKS):
+            e_send_x(sim, (CHUNKS - i) % CHUNKS)
 
     for c in perms:
         c.wait()
@@ -407,7 +421,8 @@
         return carry
 
     lax.fori_loop(0, T // 2, make_factor, 0, unroll=4)
-    for sim in range(sims):
+
+    def h_load(sim):
         for xt in range(X // 8):
             loads[sim, 1, xt].wait()
 
@@ -422,17 +437,16 @@
 
     for step in range(STEPS):
         for sim in range(sims):
-            e_arrive(sim)
-            if step > 0:
+            if step == 0:
+                h_load(sim)
+            else:
                 h_sent(sim)
+            e_arrive_y(sim)
             h_phase(sim)
-            h_send(sim)
         for sim in range(sims):
-            h_arrive(sim)
+            h_arrive_y(sim)
             e_sent(sim)
             e_phase(sim, step)
-            if step < STEPS - 1:
-                e_send(sim)
     for sim in range(sims):
         h_sent(sim)
 
@@ -521,10 +535,10 @@
             pltpu.VMEM((NS, 2, 3, T, X, 128), f32),
             pltpu.VMEM((NS, 3, T, X, 128), f32),
             pltpu.VMEM((T, X, 128), f32),
-            pltpu.VMEM((sims, 2, T, 128), f32),
-            pltpu.VMEM((sims, 2, T, 128), f32),
-            pltpu.VMEM((sims, 2, T, 128), f32),
-            pltpu.VMEM((sims, 2, T, 128), f32),
+            pltpu.VMEM((sims, CHUNKS, 2, T // CHUNKS, 128), f32),
+            pltpu.VMEM((sims, CHUNKS, 2, T // CHUNKS, 128), f32),
+            pltpu.VMEM((sims, CHUNKS, 2, T // CHUNKS, 128), f32),
+            pltpu.VMEM((sims, CHUNKS, 2, T // CHUNKS, 128), f32),
             pltpu.VMEM((2, NB, cols), f32),
             pltpu.VMEM((NB, cols), f32),
             pltpu.VMEM((n_gy, cap, cols), f32),
@@ -540,10 +554,10 @@
             dma((5,)),
             dma((sims, 2, X // 8)),
             dma((X // 8,)),
-            dma((sims,)),
-            dma((sims,)),
-            dma((sims,)),
-            dma((sims,)),
+            dma((sims, CHUNKS)),
+            dma((sims, CHUNKS)),
+            dma((sims, CHUNKS)),
+            dma((sims, CHUNKS)),
             dma((sims, 2)),
             dma((sims, 2)),
             dma((sims, 2)),

time: 45.9 us -> 44.7 us (0.974)
  Pallas kernels: 44.2 us -> 43 us
    pallas_call x1, Pallas kernels: 44.2 us -> 43 us  [per_device(): pl.pallas_call(functools.partial(kernel, n_gx, n_gy, cap), out_shape=jax....]
where the time goes in v4:
time: 44.7 us; the launch traced here: 44.6 us
  Pallas kernels  43 us (96%)
  local copies, waits for them, and re-layouts  1.57 us (4%)
    pallas_call x1, Pallas kernels, per_device(): pl.pallas_call(functools.partial(kernel, n_gx, n_gy, cap), out_shape=jax....  43 us
    unnamed x1, local copies, waits for them, and re-layouts  1.57 us

profile of v4, /device:TPU:0, one launch (start us, length us, event | category | flops | bytes accessed | tf_op | source)
XLA Modules:
  0.0 44.6 jit_solution(12602933905297814178)
XLA Ops:
  0.0 43.0 %shard_map.82 = f32[64,512]{1,0:T(8,128)} custom-call(f32[2,6,2,32,8,128]{5,4,3,2,1,0:T(8,128)} %bitcast.9, f32[2,6,2,32,8,128]{5,4,3,2,1,0:T(8,128)} %bitcast.10, f32[2,32,8,128]{3,2,1,0:T(8,128)} %bitcast.11, f32[2,4]{1,0:T(2,128)} %wave_hbm.1, s32[2,3]{1,0:T(2,128)} %cell_hbm.1, s32[4,16]{1,0:T(4,128)} %owner_hbm.1, s32[4,16]{1,0:T(4,128)} %slot_hbm.1, ...), custom_call_target="tpu_custom_call" | custom-call | tf_op jit(solution)/shard_map/pallas_call | solution.py:522
  43.0 1.6 %copy.10 = f32[64,512]{1,0:T(8,128)} copy(f32[64,512]{1,0:T(8,128)} %shard_map.82) | data formatting | bytes 262144

commit v5 on v4

--- a/solution.py
+++ b/solution.py
@@ -307,9 +307,7 @@
 
         lax.fori_loop(0, CHUNKS, body, 0)
 
-    def e_phase(sim, step):
-        s = sim % NS
-        forward = sim < NS
+    def e_phase(sim, step, forward, s):
         if forward:
             lx = cell[s, 0] - gx * X
             lyz = (cell[s, 1] - gy * (cells_yz // NZ)) * NZ + cell[s, 2]
@@ -352,10 +350,7 @@
                     else:
                         a = [asv[s, c, t] for c in range(3)]
                     term = d0 * a[0] + d1 * a[1] + d2 * a[2]
-                    if step == 2 and s == 0:
-                        D[t] = term
-                    else:
-                        D[t] = D[t] + term
+                    D[t] = D[t] + term
             else:
                 if step == 0:
                     asv[s, 0, t] = e0
@@ -366,8 +361,6 @@
                     total = D[t] + (
                         e0 * inc[s, k, 0, t] + e1 * inc[s, k, 1, t] + e2 * inc[s, k, 2, t]
                     )
-                    if step == STEPS - 1 and s == NS - 1:
-                        total = total * (f * (-1.0 / (COURANT * COURANT)))
                     D[t] = total
             return hx, hz
 
@@ -418,6 +411,8 @@
         even, odd = halves(PS[a], PS[a + T // 2])
         fac[2 * a] = (COURANT * COURANT) / even
         fac[2 * a + 1] = (COURANT * COURANT) / odd
+        D[2 * a] = zero_tile
+        D[2 * a + 1] = zero_tile
         return carry
 
     lax.fori_loop(0, T // 2, make_factor, 0, unroll=4)
@@ -439,19 +434,33 @@
         for sim in range(sims):
             if step == 0:
                 h_load(sim)
-            else:
+
+        def h_run(sim, carry):
+            if step > 0:
                 h_sent(sim)
             e_arrive_y(sim)
             h_phase(sim)
-        for sim in range(sims):
+            return carry
+
+        def e_run(forward, s, carry):
+            sim = s if forward else s + NS
             h_arrive_y(sim)
             e_sent(sim)
-            e_phase(sim, step)
+            e_phase(sim, step, forward, s)
+            return carry
+
+        lax.fori_loop(0, sims, h_run, 0)
+        lax.fori_loop(0, NS, functools.partial(e_run, True), 0)
+        lax.fori_loop(0, NS, functools.partial(e_run, False), 0)
     for sim in range(sims):
         h_sent(sim)
 
+    scale = -1.0 / (COURANT * COURANT)
+
     def d_layout(a, carry):
-        PS[a], PS[a + T // 2] = halves(D[2 * a], D[2 * a + 1])
+        PS[a], PS[a + T // 2] = halves(
+            D[2 * a] * (fac[2 * a] * scale), D[2 * a + 1] * (fac[2 * a + 1] * scale)
+        )
         return carry
 
     lax.fori_loop(0, T // 2, d_layout, 0, unroll=4)

time: 44.7 us -> 44 us (0.984)
  Pallas kernels: 43 us -> 42.3 us
    pallas_call x1, Pallas kernels: 43 us -> 42.3 us  [per_device(): pl.pallas_call(functools.partial(kernel, n_gx, n_gy, cap), out_shape=jax....]
where the time goes in v5:
time: 44 us; the launch traced here: 43.9 us
  Pallas kernels  42.3 us (96%)
  local copies, waits for them, and re-layouts  1.57 us (4%)
    pallas_call x1, Pallas kernels, per_device(): pl.pallas_call(functools.partial(kernel, n_gx, n_gy, cap), out_shape=jax....  42.3 us
    unnamed x1, local copies, waits for them, and re-layouts  1.57 us

profile of v5, /device:TPU:0, one launch (start us, length us, event | category | flops | bytes accessed | tf_op | source)
XLA Modules:
  0.0 43.9 jit_solution(17981335178026081980)
XLA Ops:
  0.0 42.3 %shard_map.82 = f32[64,512]{1,0:T(8,128)} custom-call(f32[2,6,2,32,8,128]{5,4,3,2,1,0:T(8,128)} %bitcast.9, f32[2,6,2,32,8,128]{5,4,3,2,1,0:T(8,128)} %bitcast.10, f32[2,32,8,128]{3,2,1,0:T(8,128)} %bitcast.11, f32[2,4]{1,0:T(2,128)} %wave_hbm.1, s32[2,3]{1,0:T(2,128)} %cell_hbm.1, s32[4,16]{1,0:T(4,128)} %owner_hbm.1, s32[4,16]{1,0:T(4,128)} %slot_hbm.1, ...), custom_call_target="tpu_custom_call" | custom-call | tf_op jit(solution)/shard_map/pallas_call | solution.py:531
  42.3 1.6 %copy.10 = f32[64,512]{1,0:T(8,128)} copy(f32[64,512]{1,0:T(8,128)} %shard_map.82) | data formatting | bytes 262144
